TPU v7x, 32 devices: a whole 2x2x4 slice. The times are simulated.
32 devices in a mesh: groups: 2 (over x), node: 16 (over z, y, core).
Axes of the slice: x: 2, y: 2, z: 4, core: 2. Of those that a mesh axis runs over, the one named last changes fastest.
Arguments:
- hidden: bfloat16 [4096, 4096], P(('groups', 'node')), parts along dimension 0, may hold values from -6 to 6
- queries: bfloat16 [4096, 4096], P(('groups', 'node')), parts along dimension 0, may hold values from -64 to 64
- kv_weight: bfloat16 [4096, 1024], P(None, 'node'), may hold values from -0.09375 to 0.09375
- doc_ids: int32 [4096], P('groups'), parts along dimension 0, may hold values from 0 to 2, never falling along the last dimension, each value on 1 to 1536 neighbouring positions
Outputs:
- attended: bfloat16 [4096, 4096], P(('groups', 'node')), parts along dimension 0
There are 2 independent parts, one for each index of `groups`. A program takes and returns all parts, laid end to end along the dimension named above; an argument that names none is the same for every part. Nothing has to cross between parts.
All inputs are finite; a program needn't handle non-finite values.
Results may differ from a plain program's by a relative error of at most 0.0035.
The roundings to bfloat16 on the way count: a program that leaves them out, or rounds other values in their place, can miss the bound.
Values may be sent and summed in bfloat16 or wider, within the bound.
No kernel may reach another device: no remote copies, remote signals or barrier semaphores. Data moves between devices by JAX's collectives and lax.ppermute only.
A program may use at most 128 MiB of HBM per device.

v0:
```python
import math

import jax
import jax.numpy as jnp
from jax import lax
from jax.sharding import PartitionSpec as P

KVH = 4
QPK = 8
HD = 128


def rotate_keys(keys, positions):
    half = keys.shape[-1] // 2
    freqs = 500000.0 ** (-(jnp.arange(half).astype(jnp.float32) * 2.0) / keys.shape[-1])
    angle = positions[:, None] * freqs[None, :]
    cosine = jnp.cos(angle)[:, None, :]
    sine = jnp.sin(angle)[:, None, :]
    first = keys[..., :half]
    second = keys[..., half:]
    return jnp.concatenate(
        [first * cosine - second * sine, second * cosine + first * sine], axis=-1
    )


def per_device(hidden, queries, kv_weight, doc_ids):
    rows = hidden.shape[0]
    me = lax.axis_index("node")
    first = me * rows
    columns = kv_weight.shape[1] * lax.axis_size("node")
    whole_weight = lax.all_gather(kv_weight, "node", axis=1, tiled=True)
    projected = jnp.dot(hidden, whole_weight, preferred_element_type=jnp.float32)
    split = columns // 2
    positions = (first + jnp.arange(rows)).astype(jnp.float32)
    keys = (
        rotate_keys(projected[:, :split].reshape(rows, KVH, HD), positions)
        .astype(jnp.bfloat16)
        .reshape(rows, split)
    )
    values = projected[:, split:].astype(jnp.bfloat16)
    grouped = queries.reshape(rows, KVH, QPK, HD)
    my_docs = lax.dynamic_slice_in_dim(doc_ids, first, rows)
    query_pos = first + jnp.arange(rows)
    last_query = first + rows - 1
    scale = HD ** (-0.5)

    def attend_below(limit, carry, piece, start):
        length = piece[0].shape[0]
        width = math.gcd(length, 512)

        def one_block(index, state):
            key_start = start + index * width

            def update(state):
                running, total, accum = state
                key_block = lax.dynamic_slice_in_dim(piece[0], index * width, width, 0).reshape(
                    width, KVH, HD
                )
                value_block = lax.dynamic_slice_in_dim(piece[1], index * width, width, 0).reshape(
                    width, KVH, HD
                )
                score = (
                    jnp.einsum(
                        "qgph,kgh->qgpk", grouped, key_block, preferred_element_type=jnp.float32
                    )
                    * scale
                )
                key_docs = lax.dynamic_slice_in_dim(doc_ids, key_start, width)
                key_pos = key_start + jnp.arange(width)
                mask = (my_docs[:, None] == key_docs[None, :]) & (
                    key_pos[None, :] <= query_pos[:, None]
                )
                mask = mask & (key_pos[None, :] < limit)
                mask = mask[:, None, None, :]
                score = jnp.where(mask, score, -1e30)
                newest = jnp.maximum(running, jnp.max(score, axis=-1))
                expo = jnp.where(mask, jnp.exp(score - newest[..., None]), 0.0)
                factor = jnp.exp(running - newest)
                total = total * factor + jnp.sum(expo, axis=-1)
                accum = accum * factor[..., None] + jnp.einsum(
                    "qgpk,kgh->qgph",
                    expo.astype(jnp.bfloat16),
                    value_block,
                    preferred_element_type=jnp.float32,
                )
                return (newest, total, accum)

            skip = (key_start > last_query) | (key_start >= limit)
            return lax.cond(skip, lambda s: s, update, state)

        return lax.fori_loop(0, length // width, one_block, carry)

    start_state = (
        jnp.full((rows, KVH, QPK), -1e30, jnp.float32),
        jnp.zeros((rows, KVH, QPK), jnp.float32),
        jnp.zeros((rows, KVH, QPK, HD), jnp.float32),
    )
    begin_state = attend_below(first + rows, start_state, (keys, values), first)
    running, total, accum = attend_below(
        first,
        begin_state,
        (
            lax.all_gather(keys, "node", axis=0, tiled=True),
            lax.all_gather(values, "node", axis=0, tiled=True),
        ),
        jnp.int32(0),
    )
    return (accum / total[..., None]).reshape(rows, KVH * QPK * HD).astype(jnp.bfloat16)


def solution(mesh):
    in_specs = (
        P(("groups", "node"), None),
        P(("groups", "node"), None),
        P(None, "node"),
        P("groups"),
    )
    out_specs = P(("groups", "node"), None)
    return jax.shard_map(
        per_device, mesh=mesh, in_specs=in_specs, out_specs=out_specs, check_vma=False
    )
```

profile of v0, /device:TPU:29, one launch (start us, length us, event | category | flops | bytes accessed | tf_op | source)
XLA Modules:
  0.0 222.1 jit_solution(16033873423635335971)
XLA Ops:
  7.3 75.9 %all-gather.4.cloned.1.call-done = bf16[4096,1024]{0,1:T(8,128)(2,1)} async-done(((bf16[4096,64]{0,1:T(8,128)(2,1)}), bf16[4096,1024]{0,1:T(8,128)(2,1)}) %all-gather.4.cloned.1.call-update) | async-done | bytes 8388624 | tf_op jit(solution)/shard_map/all_gather | solution.py:31
  83.2 6.3 %fusion.27 = f32[128,1024]{1,0:T(8,128)S(1)} fusion(bf16[128,4096]{1,0:T(8,128)(2,1)S(1)} %copy-done, bf16[4096,1024]{0,1:T(8,128)(2,1)} %all-gather.4.cloned.1.call-done), kind=kOutput, calls=%fused_computation.50 | convolution fusion | flops 1073741824 | bytes 9961472 | tf_op jit(solution)/shard_map/dot_general | solution.py:32
  92.0 1.6 copy.18
  95.1 1.6 broadcast_in_dim.72
  96.7 11.1 %conditional.2 = (f32[128,4,8]{0,2,1:T(8,128)S(1)}, f32[128,4,8]{0,2,1:T(8,128)S(1)}, f32[128,4,8,128]{0,3,2,1:T(8,128)}) conditional(s32[]{:T(128)} %convert_element_type.44, (s32[128]{0:T(128)S(1)}, s32[]{:T(128)}, s32[2048]{0:T(1024)}, s32[128]{0:T(128)S(1)}, s32[]{:T(128)}, /*index=5*/bf16[128,512]{0,1:T(8,128)(2,1)S(1)}, ...), branch_computations={%region_0.3_spmd, %region_3.4_spmd} | conditional | flops 276373888 | bytes 24940390 | solution.py:89
  100.1 4.7 %bitcast_add_fusion = f32[128,4,8,128]{3,0,2,1:T(8,128)} fusion(f32[128,4,8,128]{3,0,2,1:T(8,128)} %get-tuple-element.328, f32[4,128,128,8]{2,1,3,0:T(8,128)} %copy-done.1, f32[128,4,8]{0,2,1:T(8,128)S(1)} %get-tuple-element.490, f32[128,4,8]{0,2,1:T(8,128)S(1)} %max.5, pred[128,128]{0,1:T(8,128)(4,1)S(1)} %and_and_fusion, ...), kind=kOutput, calls=%fused_computation.1 | convolution fusion | flops 137887744 | bytes 6471680 | tf_op jit(solution)/shard_map/while/body/eval_jaxpr/cond/branch_0_fun/qgpk,kgh->qgph/dot_general | solution.py:80
  104.8 2.9 %copy.41 = f32[128,4,8,128]{0,3,2,1:T(8,128)} copy(f32[128,4,8,128]{3,0,2,1:T(8,128)} %bitcast_add_fusion) | data formatting | bytes 4194304 | tf_op jit(solution)/shard_map/while/body/eval_jaxpr/cond
  107.8 22.6 %all-gather.8.cloned.1.call-done = bf16[2048,512]{1,0:T(8,128)(2,1)} async-done(((bf16[128,512]{1,0:T(8,128)(2,1)}), bf16[2048,512]{1,0:T(8,128)(2,1)}) %all-gather.8.cloned.1.call-update) | async-done | bytes 2097168 | tf_op jit(solution)/shard_map/all_gather | solution.py:104
  130.4 4.0 %copy.23 = bf16[2048,512]{0,1:T(8,128)(2,1)} copy(bf16[2048,512]{1,0:T(8,128)(2,1)} %all-gather.8.cloned.1.call-done) | data formatting | bytes 4194304
  134.4 38.4 %all-gather.6.cloned.1.call-done = bf16[2048,512]{0,1:T(8,128)(2,1)} async-done(((bf16[128,512]{0,1:T(8,128)(2,1)}), bf16[2048,512]{0,1:T(8,128)(2,1)}) %all-gather.6.cloned.1.call-update) | async-done | bytes 2097168 | tf_op jit(solution)/shard_map/all_gather | solution.py:103
  172.8 39.6 %while.12 = (s32[]{:T(128)}, f32[128,4,8]{0,2,1:T(8,128)S(1)}, f32[128,4,8]{0,2,1:T(8,128)S(1)}, f32[128,4,8,128]{0,3,2,1:T(8,128)}, s32[]{:T(128)}, /*index=5*/...) while((s32[]{:T(128)}, f32[128,4,8]{0,2,1:T(8,128)S(1)}, ...), condition=%wide.region_9.0_spmd.clone.clone, body=%wide.region_4.9_spmd.clone.clone.sunk | while | flops 1102325376 | bytes 50870232 | solution.py:91
  172.8 9.9 %conditional.6 = (f32[128,4,8]{0,2,1:T(8,128)S(1)}, f32[128,4,8]{0,2,1:T(8,128)S(1)}, f32[128,4,8,128]{0,3,2,1:T(8,128)}) conditional(s32[]{:T(128)} %convert_element_type.62, (s32[128]{0:T(128)S(1)}, s32[]{:T(128)}, s32[2048]{0:T(1024)}, s32[]{:T(128)}, s32[]{:T(128)}, /*index=5*/s32[]{:T(128)}, bf16[2048,512]{0,1:T(8,128)(2,1)}, ...), branch_computations={%region_5.0_spmd, %region_8.8_spmd} | conditional | flops 1102325376 | bytes 50836664 | solution.py:89
  175.1 1.5 fusion.15
  176.6 2.1 fusion.17
  178.7 2.6 %bitcast_add_fusion.1 = f32[128,4,8,128]{0,3,2,1:T(8,128)S(1)} fusion(f32[128,4,8,128]{0,3,2,1:T(8,128)S(1)} %copy-done.2, bf16[512,4,128,1]{0,2,3,1:T(8,128)(2,1)S(1)} %bitcast.55, f32[4,512,128,8]{2,1,3,0:T(8,128)S(1)} %get-tuple-element.496, f32[128,4,8]{0,2,1:T(8,128)S(1)} %max.6, pred[128,512]{0,1:T(8,128)(4,1)S(1)} %and_and_fusion.1, ...), kind=kOutput, calls=%fused_computation.28 | convolution fusion | flops 548405248 | bytes 13205504 | tf_op jit(solution)/shard_map/while/body/eval_jaxpr/cond/branch_0_fun/qgpk,kgh->qgph/dot_general | solution.py:80
  181.3 1.4 copy-done.3
  182.7 9.9 %conditional.6 = (f32[128,4,8]{0,2,1:T(8,128)S(1)}, f32[128,4,8]{0,2,1:T(8,128)S(1)}, f32[128,4,8,128]{0,3,2,1:T(8,128)}) conditional(s32[]{:T(128)} %convert_element_type.62, (s32[128]{0:T(128)S(1)}, s32[]{:T(128)}, s32[2048]{0:T(1024)}, s32[]{:T(128)}, s32[]{:T(128)}, /*index=5*/s32[]{:T(128)}, bf16[2048,512]{0,1:T(8,128)(2,1)}, ...), branch_computations={%region_5.0_spmd, %region_8.8_spmd} | conditional | flops 1102325376 | bytes 50836664 | solution.py:89
  185.0 1.5 fusion.15
  186.5 2.1 fusion.17
  188.6 2.6 %bitcast_add_fusion.1 = f32[128,4,8,128]{0,3,2,1:T(8,128)S(1)} fusion(f32[128,4,8,128]{0,3,2,1:T(8,128)S(1)} %copy-done.2, bf16[512,4,128,1]{0,2,3,1:T(8,128)(2,1)S(1)} %bitcast.55, f32[4,512,128,8]{2,1,3,0:T(8,128)S(1)} %get-tuple-element.496, f32[128,4,8]{0,2,1:T(8,128)S(1)} %max.6, pred[128,512]{0,1:T(8,128)(4,1)S(1)} %and_and_fusion.1, ...), kind=kOutput, calls=%fused_computation.28 | convolution fusion | flops 548405248 | bytes 13205504 | tf_op jit(solution)/shard_map/while/body/eval_jaxpr/cond/branch_0_fun/qgpk,kgh->qgph/dot_general | solution.py:80
  191.2 1.4 copy-done.3
  192.6 9.9 %conditional.6 = (f32[128,4,8]{0,2,1:T(8,128)S(1)}, f32[128,4,8]{0,2,1:T(8,128)S(1)}, f32[128,4,8,128]{0,3,2,1:T(8,128)}) conditional(s32[]{:T(128)} %convert_element_type.62, (s32[128]{0:T(128)S(1)}, s32[]{:T(128)}, s32[2048]{0:T(1024)}, s32[]{:T(128)}, s32[]{:T(128)}, /*index=5*/s32[]{:T(128)}, bf16[2048,512]{0,1:T(8,128)(2,1)}, ...), branch_computations={%region_5.0_spmd, %region_8.8_spmd} | conditional | flops 1102325376 | bytes 50836664 | solution.py:89
  194.9 1.5 fusion.15
  196.4 2.1 fusion.17
  198.5 2.6 %bitcast_add_fusion.1 = f32[128,4,8,128]{0,3,2,1:T(8,128)S(1)} fusion(f32[128,4,8,128]{0,3,2,1:T(8,128)S(1)} %copy-done.2, bf16[512,4,128,1]{0,2,3,1:T(8,128)(2,1)S(1)} %bitcast.55, f32[4,512,128,8]{2,1,3,0:T(8,128)S(1)} %get-tuple-element.496, f32[128,4,8]{0,2,1:T(8,128)S(1)} %max.6, pred[128,512]{0,1:T(8,128)(4,1)S(1)} %and_and_fusion.1, ...), kind=kOutput, calls=%fused_computation.28 | convolution fusion | flops 548405248 | bytes 13205504 | tf_op jit(solution)/shard_map/while/body/eval_jaxpr/cond/branch_0_fun/qgpk,kgh->qgph/dot_general | solution.py:80
  201.1 1.4 copy-done.3
  202.5 9.9 %conditional.6 = (f32[128,4,8]{0,2,1:T(8,128)S(1)}, f32[128,4,8]{0,2,1:T(8,128)S(1)}, f32[128,4,8,128]{0,3,2,1:T(8,128)}) conditional(s32[]{:T(128)} %convert_element_type.62, (s32[128]{0:T(128)S(1)}, s32[]{:T(128)}, s32[2048]{0:T(1024)}, s32[]{:T(128)}, s32[]{:T(128)}, /*index=5*/s32[]{:T(128)}, bf16[2048,512]{0,1:T(8,128)(2,1)}, ...), branch_computations={%region_5.0_spmd, %region_8.8_spmd} | conditional | flops 1102325376 | bytes 50836664 | solution.py:89
  204.8 1.5 fusion.15
  206.3 2.1 fusion.17
  208.4 2.6 %bitcast_add_fusion.1 = f32[128,4,8,128]{0,3,2,1:T(8,128)S(1)} fusion(f32[128,4,8,128]{0,3,2,1:T(8,128)S(1)} %copy-done.2, bf16[512,4,128,1]{0,2,3,1:T(8,128)(2,1)S(1)} %bitcast.55, f32[4,512,128,8]{2,1,3,0:T(8,128)S(1)} %get-tuple-element.496, f32[128,4,8]{0,2,1:T(8,128)S(1)} %max.6, pred[128,512]{0,1:T(8,128)(4,1)S(1)} %and_and_fusion.1, ...), kind=kOutput, calls=%fused_computation.28 | convolution fusion | flops 548405248 | bytes 13205504 | tf_op jit(solution)/shard_map/while/body/eval_jaxpr/cond/branch_0_fun/qgpk,kgh->qgph/dot_general | solution.py:80
  211.0 1.4 copy-done.3
  212.4 1.8 divide_convert_fusion
  (90 shorter events, 18.7 us)
Async XLA Ops:
  6.5 76.7 %copy-start = (bf16[128,4096]{1,0:T(8,128)(2,1)S(1)}, bf16[128,4096]{1,0:T(8,128)(2,1)}, u32[]{:S(2)}) copy-start(bf16[128,4096]{1,0:T(8,128)(2,1)} %param.10) | copy-start | bytes 3145732
  6.5 76.7 %all-gather.4.cloned.1.call-start = ((), (), s32[]{:S(2)}) async-start(), calls=%async_computation | async-start | bytes 8912896 | tf_op jit(solution)/shard_map/all_gather | solution.py:31
  7.3 123.2 %all-gather.8.cloned.1.call-start = ((), (), s32[]{:S(2)}) async-start(), calls=%async_computation.2 | async-start | bytes 2228224 | tf_op jit(solution)/shard_map/all_gather | solution.py:104
  90.2 82.6 %all-gather.6.cloned.1.call-start = ((), (), s32[]{:S(2)}) async-start(), calls=%async_computation.1 | async-start | bytes 2228224 | tf_op jit(solution)/shard_map/all_gather | solution.py:103
  93.6 3.0 %copy-start.4 = (bf16[128,4,128]{0,2,1:T(8,128)(2,1)S(1)}, bf16[128,4,128]{0,2,1:T(8,128)(2,1)}, u32[]{:S(2)}) copy-start(bf16[128,4,128]{0,2,1:T(8,128)(2,1)} %copy.17) | copy-start | bytes 393220
  93.6 3.0 %copy-start.5 = (bf16[128,512]{1,0:T(8,128)(2,1)S(1)}, bf16[128,512]{1,0:T(8,128)(2,1)}, u32[]{:S(2)}) copy-start(bf16[128,512]{1,0:T(8,128)(2,1)} %slice.26) | copy-start | bytes 393220
  98.1 1.4 copy-start.1
  176.6 2.1 copy-start.2
  181.3 1.4 copy-start.3
  186.5 2.1 copy-start.2
  191.2 1.4 copy-start.3
  196.4 2.1 copy-start.2
  201.1 1.4 copy-start.3
  206.3 2.1 copy-start.2
  211.0 1.4 copy-start.3
Sparse Core Ops, SparseCore 0:
  9.5 73.6 all-gather.3
  90.3 40.0 all-gather.7
  132.6 40.1 all-gather.5
where the time goes:
time: 223 us; the launch traced here: 222 us
  waiting for transfers between devices  138 us (62%)
  local copies, waits for them, and re-layouts  30.3 us (14%)
  matrix products  27.6 us (12%)
  between operations  13.2 us (6%)
  other arithmetic  12.8 us (6%)
    all_gather x1, waiting for transfers between devices, per_device(): whole_weight = lax.all_gather(kv_weight, 'node', axis=1, tiled=True)  75.9 us
    all_gather x1, waiting for transfers between devices, per_device(): lax.all_gather(keys, 'node', axis=0, tiled=True)  38.4 us
    all_gather x1, waiting for transfers between devices, per_device(): lax.all_gather(values, 'node', axis=0, tiled=True)  22.6 us
    dot_general x5, matrix products, update(): jnp.einsum('qgpk,kgh->qgph', expo.astype(jnp.bfloat16), value_block, pref...  15.1 us
    cond x19, local copies, waits for them, and re-layouts  9.82 us
    reduce_sum x5, other arithmetic, update(): total = total * factor + jnp.sum(expo, axis=-1)  8.83 us
    dot_general x5, matrix products, update(): jnp.einsum('qgph,kgh->qgpk', grouped, key_block, preferred_element_type=j...  6.33 us
    unnamed x9, local copies, waits for them, and re-layouts  6.26 us
  transfers between devices with their start and end apart: 3, of which 3 were waited for; matrix products, arithmetic and copies ran while one was open for 9% of the time, Pallas kernels for 0%

commit v1 on v0

v1 whole, which is shorter than its diff:
```python
import math

import jax
import jax.numpy as jnp
from jax import lax
from jax.experimental import pallas as pl
from jax.experimental.pallas import tpu as pltpu
from jax.sharding import PartitionSpec as P

KVH = 4
QPK = 8
HD = 128
AXES = ("groups", "node")
MASKED = -1e30
EXP2_SCALE = HD ** (-0.5) * math.log2(math.e)
VMEM_LIMIT = 56 * 1024 * 1024

ANY = pl.BlockSpec(memory_space=pl.ANY)
IN_SMEM = pl.BlockSpec(memory_space=pltpu.SMEM)
IN_VMEM = pl.BlockSpec(memory_space=pltpu.VMEM)


def rope_tables(positions):
    half = HD // 2
    freqs = 500000.0 ** (-(jnp.arange(half).astype(jnp.float32) * 2.0) / HD)
    angle = positions.astype(jnp.float32)[:, None] * freqs[None, :]
    return jnp.cos(angle), jnp.sin(angle)


def attend_kernel(rows, chunk, n_arrays, place_ref, qdoc_ref, kdoc_ref, *refs):
    q_ref = refs[0]
    arrays = refs[1 : 1 + n_arrays]
    out_ref = refs[1 + n_arrays]
    kv, qv, acc, stat_m, stat_l, bias, sem, qsem = refs[2 + n_arrays :]
    first_chunk, end_chunk, stride = place_ref[0], place_ref[1], place_ref[2]
    me = place_ref[3]
    blocks = arrays[0].shape[1]

    q_copy = pltpu.make_async_copy(q_ref, qv, qsem)
    q_copy.start()

    def copies(a):
        base = 4 + 3 * a
        out = []
        for b in range(blocks):
            at = place_ref[base + 2] + b * stride
            out.append(
                pltpu.make_async_copy(
                    arrays[a].at[:, b],
                    kv.at[
                        place_ref[base + 1],
                        :,
                        pl.ds(pl.multiple_of(at * rows, rows), rows),
                    ],
                    sem.at[a, b],
                )
            )
        return out

    for a in range(n_arrays):

        @pl.when(place_ref[4 + 3 * a] == 1)
        def _():
            for c in copies(a):
                c.start()

    stat_m[...] = jnp.full_like(stat_m, MASKED)
    stat_l[...] = jnp.zeros_like(stat_l)
    acc[...] = jnp.zeros_like(acc)
    q_copy.wait()
    for a in range(n_arrays):

        @pl.when(place_ref[4 + 3 * a] == 1)
        def _():
            for c in copies(a):
                c.wait()

    qdoc = qdoc_ref[...]
    q_pos = me * rows + lax.broadcasted_iota(jnp.int32, (chunk, rows), 1)

    @pl.loop(first_chunk, end_chunk)
    def _(t):
        begin = pl.multiple_of(t * chunk, chunk)
        k_pos = begin + lax.broadcasted_iota(jnp.int32, (chunk, rows), 0)
        kdoc = kdoc_ref[pl.ds(begin, chunk), :]
        seen = (k_pos <= q_pos) & (kdoc == qdoc)
        bias[...] = jnp.where(seen, 0.0, MASKED)
        for g in range(KVH):
            keys = kv[g % 2, g // 2, pl.ds(begin, chunk), :]
            values_t = kv[g % 2, 2 + g // 2, pl.ds(begin, chunk), :].T
            for p in range(QPK):
                h = g * QPK + p
                query = qv[:, h * HD : (h + 1) * HD]
                score = lax.dot_general(
                    keys, query, (((1,), (1,)), ((), ())), preferred_element_type=jnp.float32
                )
                score = score + bias[...]
                old = stat_m[h : h + 1, :]
                top = jnp.maximum(old, jnp.max(score, axis=0, keepdims=True))
                expo = jnp.exp2((score - top) * EXP2_SCALE)
                factor = jnp.exp2((old - top) * EXP2_SCALE)
                stat_m[h : h + 1, :] = top
                stat_l[h : h + 1, :] = stat_l[h : h + 1, :] * factor + jnp.sum(
                    expo, axis=0, keepdims=True
                )
                part = jnp.dot(
                    values_t, expo.astype(jnp.bfloat16), preferred_element_type=jnp.float32
                )
                acc[h] = acc[h] * factor + part

    for h in range(KVH * QPK):
        whole = acc[h] / stat_l[h : h + 1, :]
        out_ref[:, h * HD : (h + 1) * HD] = whole.T.astype(jnp.bfloat16)


def attend(queries, doc_ids, me, arrays, places, stride):
    rows = queries.shape[0]
    tokens = doc_ids.shape[0]
    chunk = math.gcd(tokens, 512)
    my_docs = lax.dynamic_slice_in_dim(doc_ids, me * rows, rows)
    first_key = jnp.sum((doc_ids < my_docs[0]).astype(jnp.int32))
    heads = [first_key // chunk, (me * rows + rows + chunk - 1) // chunk, stride, me]
    for used, kind, at in places:
        heads += [used, kind, at]
    place = jnp.stack([jnp.asarray(v).astype(jnp.int32) for v in heads])
    n = len(arrays)
    qdoc = my_docs.reshape(1, rows)
    kdoc = jnp.broadcast_to(doc_ids.reshape(tokens, 1), (tokens, HD))
    return pl.pallas_call(
        lambda *refs: attend_kernel(rows, chunk, n, *refs),
        out_shape=jax.ShapeDtypeStruct(queries.shape, jnp.bfloat16),
        in_specs=[IN_SMEM, IN_VMEM, IN_VMEM, ANY] + [ANY] * n,
        out_specs=IN_VMEM,
        scratch_shapes=[
            pltpu.VMEM((2, KVH, tokens, HD), jnp.bfloat16),
            pltpu.VMEM(queries.shape, jnp.bfloat16),
            pltpu.VMEM((KVH * QPK, HD, rows), jnp.float32),
            pltpu.VMEM((KVH * QPK, rows), jnp.float32),
            pltpu.VMEM((KVH * QPK, rows), jnp.float32),
            pltpu.VMEM((chunk, rows), jnp.float32),
            pltpu.SemaphoreType.DMA((n, arrays[0].shape[1])),
            pltpu.SemaphoreType.DMA,
        ],
        compiler_params=pltpu.CompilerParams(vmem_limit_bytes=VMEM_LIMIT),
        cost_estimate=pl.CostEstimate(
            flops=2 * rows * tokens * HD * KVH * QPK * 2,
            bytes_accessed=8 * 1024 * 1024,
            transcendentals=rows * tokens * KVH * QPK,
        ),
        name="attend",
    )(place, qdoc, kdoc, queries, *arrays)


def project_kernel(rows, n_pieces, place_ref, cos_ref, sin_ref, *refs):
    hidden = refs[:2]
    pieces = refs[2 : 2 + n_pieces]
    out_ref = refs[2 + n_pieces]
    hbuf, wbuf, hsem, wsem = refs[3 + n_pieces :]
    half = HD // 2
    started = []
    for i in range(2):
        at = place_ref[0] if i == 0 else rows - place_ref[0]
        started.append(
            pltpu.make_async_copy(
                hidden[i], hbuf.at[pl.ds(pl.multiple_of(at, rows), rows)], hsem.at[i]
            )
        )
    for i in range(n_pieces):
        size = pieces[i].shape[0]
        started.append(
            pltpu.make_async_copy(
                pieces[i],
                wbuf.at[pl.ds(pl.multiple_of(place_ref[5 + i], size), size)],
                wsem.at[i],
            )
        )
    for c in started:
        c.start()
    for c in started:
        c.wait()
    for pair in range(2):
        both = lax.dot_general(
            hbuf[...],
            wbuf[pair * 2 * HD : (pair + 1) * 2 * HD, :],
            (((1,), (1,)), ((), ())),
            preferred_element_type=jnp.float32,
        )
        for s in range(2):
            head = place_ref[1 + pair * 2 + s]
            a = both[:, s * HD : s * HD + half]
            b = both[:, s * HD + half : (s + 1) * HD]
            kind = head // 2
            cosine = cos_ref[kind]
            sine = sin_ref[kind]
            turned = jnp.concatenate([a * cosine - b * sine, b * cosine + a * sine], axis=-1)
            out_ref[head] = turned.astype(jnp.bfloat16).reshape(2, rows, HD)


def project(hidden, other, row, slots, pieces, cos, sin):
    rows, depth = hidden.shape
    place = [row] + list(slots) + [at for _, at in pieces]
    place = jnp.stack([jnp.asarray(v).astype(jnp.int32) for v in place])
    n = len(pieces)
    return pl.pallas_call(
        lambda *refs: project_kernel(rows, n, *refs),
        out_shape=jax.ShapeDtypeStruct((4, 2, rows, HD), jnp.bfloat16),
        in_specs=[IN_SMEM, IN_VMEM, IN_VMEM] + [ANY] * (2 + n),
        out_specs=IN_VMEM,
        scratch_shapes=[
            pltpu.VMEM((2 * rows, depth), jnp.bfloat16),
            pltpu.VMEM((4 * HD, depth), jnp.bfloat16),
            pltpu.SemaphoreType.DMA((2,)),
            pltpu.SemaphoreType.DMA((n,)),
        ],
        compiler_params=pltpu.CompilerParams(vmem_limit_bytes=VMEM_LIMIT),
        cost_estimate=pl.CostEstimate(
            flops=2 * 2 * rows * depth * 4 * HD,
            bytes_accessed=7 * 1024 * 1024,
            transcendentals=0,
        ),
        name="project",
    )(place, cos, sin, hidden, other, *[p for p, _ in pieces])


def by_planes(hidden, queries, kv_weight, doc_ids):
    rows = hidden.shape[0]
    width = kv_weight.shape[1]
    x = lax.axis_index("groups")
    node = lax.axis_index("node")
    z, y, c = node // 4, (node // 2) % 2, node % 2

    def hop(fn):
        pairs = []
        for i in range(32):
            to = fn(i // 16, (i // 4) % 4, (i // 2) % 2, i % 2)
            if to is not None:
                pairs.append((i, ((to[0] * 4 + to[1]) * 2 + to[2]) * 2 + to[3]))
        return lambda v: lax.ppermute(v, AXES, pairs)

    to_core = hop(lambda x, z, y, c: (x, z, y, 1 - c))
    to_y = hop(lambda x, z, y, c: (x, z, 1 - y, c))
    to_x = hop(lambda x, z, y, c: (1 - x, z, y, c))
    to_z = {k: hop(lambda x, z, y, c, k=k: (x, z ^ k, y, c)) for k in (1, 2, 3)}
    up = {
        k: hop(lambda x, z, y, c, k=k: (x, z + k, y, c) if z + k < 4 else None) for k in (1, 2, 3)
    }

    weight = kv_weight.T
    part = width // 2
    mine = lax.dynamic_slice_in_dim(weight, x * part, part, 0)
    from_z = {k: to_z[k](mine) for k in (3, 2, 1)}
    other_hidden = to_y(hidden)
    pieces = [(weight, c * width), (to_core(weight), (1 - c) * width)]
    for k in (3, 2, 1):
        base = k * HD
        w = from_z[k]
        w_x = to_x(w)
        pieces.append((w, base + c * width + x * part))
        pieces.append((w_x, base + c * width + (1 - x) * part))
        pieces.append((to_core(w), base + (1 - c) * width + x * part))
        pieces.append((to_core(w_x), base + (1 - c) * width + (1 - x) * part))

    token_blocks = 4 * z + 2 * jnp.arange(2) + c
    positions = (token_blocks[:, None] * rows + jnp.arange(rows)[None, :]).reshape(-1)
    cosine, sine = rope_tables(positions)
    cos = jnp.stack([cosine, jnp.ones_like(cosine)])
    sin = jnp.stack([sine, jnp.zeros_like(sine)])
    kv = project(hidden, other_hidden, y * rows, [z ^ k for k in range(4)], pieces, cos, sin)

    arrays, places = [], []
    for k in range(4):
        below = kv if k == 0 else up[k](kv)
        across = to_y(below)
        used = z - k >= 0
        at = 4 * jnp.maximum(z - k, 0)
        for array, kind, core in (
            (below, y, c),
            (to_core(below), y, 1 - c),
            (across, 1 - y, c),
            (to_core(across), 1 - y, 1 - c),
        ):
            arrays.append(array)
            places.append((used, kind, at + core))
    return attend(queries, doc_ids, node, arrays, places, 2)


def by_gathers(hidden, queries, kv_weight, doc_ids):
    rows = hidden.shape[0]
    me = lax.axis_index("node")
    whole = lax.all_gather(kv_weight, "node", axis=1, tiled=True)
    projected = jnp.dot(hidden, whole, preferred_element_type=jnp.float32)
    split = whole.shape[1] // 2
    cosine, sine = rope_tables(me * rows + jnp.arange(rows))
    keys = projected[:, :split].reshape(rows, KVH, HD)
    a, b = keys[..., : HD // 2], keys[..., HD // 2 :]
    cosine, sine = cosine[:, None, :], sine[:, None, :]
    keys = jnp.concatenate([a * cosine - b * sine, b * cosine + a * sine], axis=-1)
    both = jnp.concatenate([keys, projected[:, split:].reshape(rows, KVH, HD)], axis=1)
    both = both.astype(jnp.bfloat16).transpose(1, 0, 2)
    whole = lax.all_gather(both, "node", axis=1, tiled=True)
    tokens = whole.shape[1]
    whole = whole.reshape(2, 2, 2, tokens // rows, rows, HD)
    arrays = [whole[:, :, kind].reshape(4, tokens // rows, rows, HD) for kind in range(2)]
    return attend(queries, doc_ids, me, arrays, [(1, 0, 0), (1, 1, 0)], 1)


def solution(mesh):
    planes = mesh.shape["groups"] == 2 and mesh.shape["node"] == 16
    in_specs = (P(AXES, None), P(AXES, None), P(None, "node"), P("groups"))
    return jax.shard_map(
        by_planes if planes else by_gathers,
        mesh=mesh,
        in_specs=in_specs,
        out_specs=P(AXES, None),
        check_vma=False,
    )
```

time: 223 us -> 115 us (0.52)
  the two profiles are of different devices: /device:TPU:29 before, /device:TPU:17 now
where the time goes in v1:
time: 115 us; the launch traced here: 113 us
  starting transfers between devices  40.2 us (35%)
  waiting for transfers between devices  36.7 us (32%)
  Pallas kernels  21.9 us (19%)
  local copies, waits for them, and re-layouts  9.95 us (9%)
  between operations  2.89 us (3%)
  other arithmetic  1.29 us (1%)
    ppermute x29, starting transfers between devices, hop(): return lambda v: lax.ppermute(v, AXES, pairs)  40.2 us
    ppermute x29, waiting for transfers between devices, hop(): return lambda v: lax.ppermute(v, AXES, pairs)  36.7 us
    pallas_call x1, Pallas kernels, attend(): pl.pallas_call(lambda *refs: attend_kernel(rows, chunk, n, *refs), out_sh...  15.7 us
    pallas_call x1, Pallas kernels, project(): pl.pallas_call(lambda *refs: project_kernel(rows, n, *refs), out_shape=ja...  6.19 us
    unnamed x52, local copies, waits for them, and re-layouts  4.02 us
  transfers between devices with their start and end apart: 29, of which 7 were waited for; matrix products, arithmetic and copies ran while one was open for 4% of the time, Pallas kernels for 0%

profile of v1, /device:TPU:17, one launch (start us, length us, event | category | flops | bytes accessed | tf_op | source)
XLA Modules:
  0.0 113.0 jit_solution(1571477574608130700)
XLA Ops:
  0.0 1.0 dynamic-slice_bitcast_fusion
  1.0 1.4 %collective-permute-start.10 = (bf16[32,4096]{1,0:T(8,128)(2,1)S(1)}, bf16[32,4096]{1,0:T(8,128)(2,1)S(1)}, u32[]{:S(2)}, u32[]{:S(2)}) collective-permute-start(bf16[32,4096]{1,0:T(8,128)(2,1)S(1)} %dynamic-slice_bitcast_fusion), channel_id=1, source_target_pairs={{0,4},{1,5},{2,6},{3,7},{4,0},{5,1},{6,2},{7,3},{8,12},{9,13},{10,... | collective-permute-start | bytes 786440 | tf_op jit(solution)/shard_map/ppermute | solution.py:238
  2.4 2.2 %collective-permute-start.6 = (bf16[32,4096]{1,0:T(8,128)(2,1)S(1)}, bf16[32,4096]{1,0:T(8,128)(2,1)S(1)}, u32[]{:S(2)}, u32[]{:S(2)}) collective-permute-start(bf16[32,4096]{1,0:T(8,128)(2,1)S(1)} %dynamic-slice_bitcast_fusion), channel_id=1, source_target_pairs={{0,8},{1,9},{2,10},{3,11},{4,12},{5,13},{6,14},{7,15},{8,0},{9,1},... | collective-permute-start | bytes 786440 | tf_op jit(solution)/shard_map/ppermute | solution.py:238
  4.7 1.2 %collective-permute-start = (bf16[128,4096]{1,0:T(8,128)(2,1)}, bf16[128,4096]{1,0:T(8,128)(2,1)S(1)}, u32[]{:S(2)}, u32[]{:S(2)}) collective-permute-start(bf16[128,4096]{1,0:T(8,128)(2,1)} %refs_3_.2), channel_id=1, source_target_pairs={{0,2},{1,3},{2,0},{3,1},{4,6},{5,7},{6,4},{7,5},{8,10},{9,11},{10,... | collective-permute-start | bytes 3145736 | tf_op jit(solution)/shard_map/ppermute | solution.py:238
  5.9 2.4 %collective-permute-done.10.refs_15_ = bf16[32,4096]{1,0:T(8,128)(2,1)S(1)} collective-permute-done((bf16[32,4096]{1,0:T(8,128)(2,1)S(1)}, bf16[32,4096]{1,0:T(8,128)(2,1)S(1)}, u32[]{:S(2)}, u32[]{:S(2)}) %collective-permute-start.10) | collective-permute-done | bytes 262176 | tf_op jit(solution)/shard_map/ppermute | solution.py:238
  8.3 1.2 %collective-permute-start.11 = (bf16[32,4096]{1,0:T(8,128)(2,1)S(1)}, bf16[32,4096]{1,0:T(8,128)(2,1)S(1)}, u32[]{:S(2)}, u32[]{:S(2)}) collective-permute-start(bf16[32,4096]{1,0:T(8,128)(2,1)S(1)} %collective-permute-done.10.refs_15_), channel_id=1, source_target_pairs={{0,16},{1,17},{2,18},{3,19},{4,20},{5,21},{6,22},{7,23},{8,24},{9,... | collective-permute-start | bytes 786440 | tf_op jit(solution)/shard_map/ppermute | solution.py:238
  9.5 0.9 collective-permute-done.2.refs_7_
  10.4 1.2 %collective-permute-start.3 = (bf16[32,4096]{1,0:T(8,128)(2,1)S(1)}, bf16[32,4096]{1,0:T(8,128)(2,1)S(1)}, u32[]{:S(2)}, u32[]{:S(2)}) collective-permute-start(bf16[32,4096]{1,0:T(8,128)(2,1)S(1)} %collective-permute-done.2.refs_7_), channel_id=1, source_target_pairs={{0,16},{1,17},{2,18},{3,19},{4,20},{5,21},{6,22},{7,23},{8,24},{9,... | collective-permute-start | bytes 786440 | tf_op jit(solution)/shard_map/ppermute | solution.py:238
  11.6 12.7 %collective-permute-done.6.refs_11_ = bf16[32,4096]{1,0:T(8,128)(2,1)S(1)} collective-permute-done((bf16[32,4096]{1,0:T(8,128)(2,1)S(1)}, bf16[32,4096]{1,0:T(8,128)(2,1)S(1)}, u32[]{:S(2)}, u32[]{:S(2)}) %collective-permute-start.6) | collective-permute-done | bytes 262176 | tf_op jit(solution)/shard_map/ppermute | solution.py:238
  24.2 1.2 %collective-permute-start.7 = (bf16[32,4096]{1,0:T(8,128)(2,1)S(1)}, bf16[32,4096]{1,0:T(8,128)(2,1)S(1)}, u32[]{:S(2)}, u32[]{:S(2)}) collective-permute-start(bf16[32,4096]{1,0:T(8,128)(2,1)S(1)} %collective-permute-done.6.refs_11_), channel_id=1, source_target_pairs={{0,16},{1,17},{2,18},{3,19},{4,20},{5,21},{6,22},{7,23},{8,24},{9,... | collective-permute-start | bytes 786440 | tf_op jit(solution)/shard_map/ppermute | solution.py:238
  25.5 1.8 %collective-permute-start.12 = (bf16[32,4096]{1,0:T(8,128)(2,1)S(1)}, bf16[32,4096]{1,0:T(8,128)(2,1)S(1)}, u32[]{:S(2)}, u32[]{:S(2)}) collective-permute-start(bf16[32,4096]{1,0:T(8,128)(2,1)S(1)} %collective-permute-done.10.refs_15_), channel_id=1, source_target_pairs={{0,1},{1,0},{2,3},{3,2},{4,5},{5,4},{6,7},{7,6},{8,9},{9,8},{10,11... | collective-permute-start | bytes 786440 | tf_op jit(solution)/shard_map/ppermute | solution.py:238
  27.4 5.6 %collective-permute-start.8 = (bf16[32,4096]{1,0:T(8,128)(2,1)S(1)}, bf16[32,4096]{1,0:T(8,128)(2,1)S(1)}, u32[]{:S(2)}, u32[]{:S(2)}) collective-permute-start(bf16[32,4096]{1,0:T(8,128)(2,1)S(1)} %collective-permute-done.6.refs_11_), channel_id=1, source_target_pairs={{0,1},{1,0},{2,3},{3,2},{4,5},{5,4},{6,7},{7,6},{8,9},{9,8},{10,11... | collective-permute-start | bytes 786440 | tf_op jit(solution)/shard_map/ppermute | solution.py:238
  33.7 2.8 %collective-permute-start.1 = (bf16[64,4096]{1,0:T(8,128)(2,1)S(1)}, bf16[64,4096]{1,0:T(8,128)(2,1)S(1)}, u32[]{:S(2)}, u32[]{:S(2)}) collective-permute-start(bf16[64,4096]{1,0:T(8,128)(2,1)S(1)} %bitcast.46), channel_id=1, source_target_pairs={{0,1},{1,0},{2,3},{3,2},{4,5},{5,4},{6,7},{7,6},{8,9},{9,8},{10,11... | collective-permute-start | bytes 1572872 | tf_op jit(solution)/shard_map/ppermute | solution.py:238
  38.5 0.7 stack.210.refs_1_
  41.4 1.0 copy-done.1
  42.4 6.2 %project.1.refs_4_ = bf16[4,2,128,128]{3,2,1,0:T(8,128)(2,1)} custom-call(s32[19]{0:T(128)} %stack.209.refs_0_, f32[2,256,64]{2,1,0:T(8,128)} %stack.210.refs_1_, f32[2,256,64]{2,1,0:T(8,128)} %stack.211.refs_2_, bf16[128,4096]{1,0:T(8,128)(2,1)} %refs_3_.2, bf16[128,4096]{1,0:T(8,128)(2,1)} %copy-done.1, bf16[64,4096]{1,0:T(8,128)(2,1)} %bitcast.45, ...), custom_call_target="tpu_custom_call" | custom-call | flops 1073741824 | bytes 7340032 | tf_op jit(solution)/shard_map/project/pallas_call | solution.py:204
  48.6 2.2 %collective-permute-start.17 = (bf16[4,2,128,128]{3,2,1,0:T(8,128)(2,1)}, bf16[4,2,128,128]{3,2,1,0:T(8,128)(2,1)S(1)}, u32[]{:S(2)}, u32[]{:S(2)}) collective-permute-start(bf16[4,2,128,128]{3,2,1,0:T(8,128)(2,1)} %project.1.refs_4_), channel_id=1, source_target_pairs={{0,4},{1,5},{2,6},{3,7},{4,8},{5,9},{6,10},{7,11},{8,12},{9,13},{1... | collective-permute-start | bytes 786440 | tf_op jit(solution)/shard_map/ppermute | solution.py:238
  50.8 1.3 %collective-permute-start.21 = (bf16[4,2,128,128]{3,2,1,0:T(8,128)(2,1)}, bf16[4,2,128,128]{3,2,1,0:T(8,128)(2,1)S(1)}, u32[]{:S(2)}, u32[]{:S(2)}) collective-permute-start(bf16[4,2,128,128]{3,2,1,0:T(8,128)(2,1)} %project.1.refs_4_), channel_id=1, source_target_pairs={{0,8},{1,9},{2,10},{3,11},{4,12},{5,13},{6,14},{7,15},{16,24},{17,... | collective-permute-start | bytes 786440 | tf_op jit(solution)/shard_map/ppermute | solution.py:238
  52.8 1.3 %collective-permute-start.15 = (bf16[4,2,128,128]{3,2,1,0:T(8,128)(2,1)}, bf16[4,2,128,128]{3,2,1,0:T(8,128)(2,1)S(1)}, u32[]{:S(2)}, u32[]{:S(2)}) collective-permute-start(bf16[4,2,128,128]{3,2,1,0:T(8,128)(2,1)} %project.1.refs_4_), channel_id=1, source_target_pairs={{0,2},{1,3},{2,0},{3,1},{4,6},{5,7},{6,4},{7,5},{8,10},{9,11},{10,... | collective-permute-start | bytes 786440 | tf_op jit(solution)/shard_map/ppermute | solution.py:238
  54.6 15.3 %collective-permute-done.17.refs_8_ = bf16[4,2,128,128]{3,2,1,0:T(8,128)(2,1)S(1)} collective-permute-done((bf16[4,2,128,128]{3,2,1,0:T(8,128)(2,1)}, bf16[4,2,128,128]{3,2,1,0:T(8,128)(2,1)S(1)}, u32[]{:S(2)}, u32[]{:S(2)}) %collective-permute-start.17) | collective-permute-done | bytes 262176 | tf_op jit(solution)/shard_map/ppermute | solution.py:238
  69.9 1.2 %collective-permute-start.19 = (bf16[4,2,128,128]{3,2,1,0:T(8,128)(2,1)S(1)}, bf16[4,2,128,128]{3,2,1,0:T(8,128)(2,1)S(1)}, u32[]{:S(2)}, u32[]{:S(2)}) collective-permute-start(bf16[4,2,128,128]{3,2,1,0:T(8,128)(2,1)S(1)} %collective-permute-done.17.refs_8_), channel_id=1, source_target_pairs={{0,2},{1,3},{2,0},{3,1},{4,6},{5,7},{6,4},{7,5},{8,10},{9,11},{10,... | collective-permute-start | bytes 786440 | tf_op jit(solution)/shard_map/ppermute | solution.py:238
  71.4 1.2 %collective-permute-start.27 = (bf16[4,2,128,128]{3,2,1,0:T(8,128)(2,1)S(1)}, bf16[4,2,128,128]{3,2,1,0:T(8,128)(2,1)S(1)}, u32[]{:S(2)}, u32[]{:S(2)}) collective-permute-start(bf16[4,2,128,128]{3,2,1,0:T(8,128)(2,1)S(1)} %collective-permute-done.25.refs_16_), channel_id=1, source_target_pairs={{0,2},{1,3},{2,0},{3,1},{4,6},{5,7},{6,4},{7,5},{8,10},{9,11},{10,... | collective-permute-start | bytes 786440 | tf_op jit(solution)/shard_map/ppermute | solution.py:238
  72.6 2.0 %collective-permute-start.16 = (bf16[4,2,128,128]{3,2,1,0:T(8,128)(2,1)S(1)}, bf16[4,2,128,128]{3,2,1,0:T(8,128)(2,1)S(1)}, u32[]{:S(2)}, u32[]{:S(2)}) collective-permute-start(bf16[4,2,128,128]{3,2,1,0:T(8,128)(2,1)S(1)} %collective-permute-done.15.refs_6_), channel_id=1, source_target_pairs={{0,1},{1,0},{2,3},{3,2},{4,5},{5,4},{6,7},{7,6},{8,9},{9,8},{10,11... | collective-permute-start | bytes 786440 | tf_op jit(solution)/shard_map/ppermute | solution.py:238
  74.7 1.8 %collective-permute-done.19.refs_10_ = bf16[4,2,128,128]{3,2,1,0:T(8,128)(2,1)S(1)} collective-permute-done((bf16[4,2,128,128]{3,2,1,0:T(8,128)(2,1)S(1)}, bf16[4,2,128,128]{3,2,1,0:T(8,128)(2,1)S(1)}, u32[]{:S(2)}, u32[]{:S(2)}) %collective-permute-start.19) | collective-permute-done | bytes 262176 | tf_op jit(solution)/shard_map/ppermute | solution.py:238
  76.5 3.8 %collective-permute-start.22 = (bf16[4,2,128,128]{3,2,1,0:T(8,128)(2,1)S(1)}, bf16[4,2,128,128]{3,2,1,0:T(8,128)(2,1)S(1)}, u32[]{:S(2)}, u32[]{:S(2)}) collective-permute-start(bf16[4,2,128,128]{3,2,1,0:T(8,128)(2,1)S(1)} %collective-permute-done.21.refs_12_), channel_id=1, source_target_pairs={{0,1},{1,0},{2,3},{3,2},{4,5},{5,4},{6,7},{7,6},{8,9},{9,8},{10,11... | collective-permute-start | bytes 786440 | tf_op jit(solution)/shard_map/ppermute | solution.py:238
  80.3 1.8 %collective-permute-done.23.refs_14_ = bf16[4,2,128,128]{3,2,1,0:T(8,128)(2,1)S(1)} collective-permute-done((bf16[4,2,128,128]{3,2,1,0:T(8,128)(2,1)S(1)}, bf16[4,2,128,128]{3,2,1,0:T(8,128)(2,1)S(1)}, u32[]{:S(2)}, u32[]{:S(2)}) %collective-permute-start.23) | collective-permute-done | bytes 262176 | tf_op jit(solution)/shard_map/ppermute | solution.py:238
  82.1 3.8 %collective-permute-start.26 = (bf16[4,2,128,128]{3,2,1,0:T(8,128)(2,1)S(1)}, bf16[4,2,128,128]{3,2,1,0:T(8,128)(2,1)S(1)}, u32[]{:S(2)}, u32[]{:S(2)}) collective-permute-start(bf16[4,2,128,128]{3,2,1,0:T(8,128)(2,1)S(1)} %collective-permute-done.25.refs_16_), channel_id=1, source_target_pairs={{0,1},{1,0},{2,3},{3,2},{4,5},{5,4},{6,7},{7,6},{8,9},{9,8},{10,11... | collective-permute-start | bytes 786440 | tf_op jit(solution)/shard_map/ppermute | solution.py:238
  85.9 1.8 %collective-permute-done.27.refs_18_ = bf16[4,2,128,128]{3,2,1,0:T(8,128)(2,1)S(1)} collective-permute-done((bf16[4,2,128,128]{3,2,1,0:T(8,128)(2,1)S(1)}, bf16[4,2,128,128]{3,2,1,0:T(8,128)(2,1)S(1)}, u32[]{:S(2)}, u32[]{:S(2)}) %collective-permute-start.27) | collective-permute-done | bytes 262176 | tf_op jit(solution)/shard_map/ppermute | solution.py:238
  87.8 2.1 %collective-permute-start.20 = (bf16[4,2,128,128]{3,2,1,0:T(8,128)(2,1)S(1)}, bf16[4,2,128,128]{3,2,1,0:T(8,128)(2,1)S(1)}, u32[]{:S(2)}, u32[]{:S(2)}) collective-permute-start(bf16[4,2,128,128]{3,2,1,0:T(8,128)(2,1)S(1)} %collective-permute-done.19.refs_10_), channel_id=1, source_target_pairs={{0,1},{1,0},{2,3},{3,2},{4,5},{5,4},{6,7},{7,6},{8,9},{9,8},{10,11... | collective-permute-start | bytes 786440 | tf_op jit(solution)/shard_map/ppermute | solution.py:238
  94.4 0.7 stack.189.refs_0_
  95.8 1.3 %broadcast_in_dim.2.refs_2_ = s32[2048,128]{1,0:T(8,128)} broadcast(s32[2048]{0:T(1024)S(1)} %copy-done.12), dimensions={0} | broadcast | bytes 1056768 | tf_op jit(solution)/shard_map/broadcast_in_dim | solution.py:128
  97.3 15.7 %attend.1 = bf16[128,4096]{1,0:T(8,128)(2,1)} custom-call(s32[52]{0:T(128)} %stack.189.refs_0_, s32[1,128]{1,0:T(1,128)} %dynamic-slice_bitcast_fusion.1.refs_1_, s32[2048,128]{1,0:T(8,128)} %broadcast_in_dim.2.refs_2_, bf16[128,4096]{1,0:T(8,128)(2,1)} %refs_3_.3, bf16[4,2,128,128]{3,2,1,0:T(8,128)(2,1)} %project.1.refs_4_, ...), custom_call_target="tpu_custom_call" | custom-call | flops 4294967296 | bytes 8388608 | tf_op jit(solution)/shard_map/attend/pallas_call | solution.py:129
  (93 shorter events, 9.1 us)
Async XLA Ops:
  0.0 33.7 %copy-start = (bf16[4096,64]{0,1:T(8,128)(2,1)S(1)}, bf16[4096,64]{0,1:T(8,128)(2,1)}, u32[]{:S(2)}) copy-start(bf16[4096,64]{0,1:T(8,128)(2,1)} %param.6) | copy-start | bytes 1572868
  1.0 7.2 %collective-permute-start.10 = (bf16[32,4096]{1,0:T(8,128)(2,1)S(1)}, bf16[32,4096]{1,0:T(8,128)(2,1)S(1)}, u32[]{:S(2)}, u32[]{:S(2)}) collective-permute-start(bf16[32,4096]{1,0:T(8,128)(2,1)S(1)} %dynamic-slice_bitcast_fusion), channel_id=1, source_target_pairs={{0,4},{1,5},{2,6},{3,7},{4,0},{5,1},{6,2},{7,3},{8,12},{9,13},{10,... | collective-permute-start | bytes 786440 | tf_op jit(solution)/shard_map/ppermute | solution.py:238
  2.4 7.9 %collective-permute-start.2 = (bf16[32,4096]{1,0:T(8,128)(2,1)S(1)}, bf16[32,4096]{1,0:T(8,128)(2,1)S(1)}, u32[]{:S(2)}, u32[]{:S(2)}) collective-permute-start(bf16[32,4096]{1,0:T(8,128)(2,1)S(1)} %dynamic-slice_bitcast_fusion), channel_id=1, source_target_pairs={{0,12},{1,13},{2,14},{3,15},{4,8},{5,9},{6,10},{7,11},{8,4},{9,5},... | collective-permute-start | bytes 786440 | tf_op jit(solution)/shard_map/ppermute | solution.py:238
  2.4 21.8 %collective-permute-start.6 = (bf16[32,4096]{1,0:T(8,128)(2,1)S(1)}, bf16[32,4096]{1,0:T(8,128)(2,1)S(1)}, u32[]{:S(2)}, u32[]{:S(2)}) collective-permute-start(bf16[32,4096]{1,0:T(8,128)(2,1)S(1)} %dynamic-slice_bitcast_fusion), channel_id=1, source_target_pairs={{0,8},{1,9},{2,10},{3,11},{4,12},{5,13},{6,14},{7,15},{8,0},{9,1},... | collective-permute-start | bytes 786440 | tf_op jit(solution)/shard_map/ppermute | solution.py:238
  4.7 36.0 %collective-permute-start = (bf16[128,4096]{1,0:T(8,128)(2,1)}, bf16[128,4096]{1,0:T(8,128)(2,1)S(1)}, u32[]{:S(2)}, u32[]{:S(2)}) collective-permute-start(bf16[128,4096]{1,0:T(8,128)(2,1)} %refs_3_.2), channel_id=1, source_target_pairs={{0,2},{1,3},{2,0},{3,1},{4,6},{5,7},{6,4},{7,5},{8,10},{9,11},{10,... | collective-permute-start | bytes 3145736 | tf_op jit(solution)/shard_map/ppermute | solution.py:238
  8.3 30.9 %copy-start.3 = (bf16[32,4096]{1,0:T(8,128)(2,1)}, bf16[32,4096]{1,0:T(8,128)(2,1)S(1)}, u32[]{:S(2)}) copy-start(bf16[32,4096]{1,0:T(8,128)(2,1)S(1)} %collective-permute-done.10.refs_15_) | copy-start | bytes 786436
  8.3 19.0 %collective-permute-start.11 = (bf16[32,4096]{1,0:T(8,128)(2,1)S(1)}, bf16[32,4096]{1,0:T(8,128)(2,1)S(1)}, u32[]{:S(2)}, u32[]{:S(2)}) collective-permute-start(bf16[32,4096]{1,0:T(8,128)(2,1)S(1)} %collective-permute-done.10.refs_15_), channel_id=1, source_target_pairs={{0,16},{1,17},{2,18},{3,19},{4,20},{5,21},{6,22},{7,23},{8,24},{9,... | collective-permute-start | bytes 786440 | tf_op jit(solution)/shard_map/ppermute | solution.py:238
  10.3 28.9 %copy-start.4 = (bf16[32,4096]{1,0:T(8,128)(2,1)}, bf16[32,4096]{1,0:T(8,128)(2,1)S(1)}, u32[]{:S(2)}) copy-start(bf16[32,4096]{1,0:T(8,128)(2,1)S(1)} %collective-permute-done.2.refs_7_) | copy-start | bytes 786436
  10.4 17.0 %collective-permute-start.3 = (bf16[32,4096]{1,0:T(8,128)(2,1)S(1)}, bf16[32,4096]{1,0:T(8,128)(2,1)S(1)}, u32[]{:S(2)}, u32[]{:S(2)}) collective-permute-start(bf16[32,4096]{1,0:T(8,128)(2,1)S(1)} %collective-permute-done.2.refs_7_), channel_id=1, source_target_pairs={{0,16},{1,17},{2,18},{3,19},{4,20},{5,21},{6,22},{7,23},{8,24},{9,... | collective-permute-start | bytes 786440 | tf_op jit(solution)/shard_map/ppermute | solution.py:238
  24.2 8.7 %collective-permute-start.7 = (bf16[32,4096]{1,0:T(8,128)(2,1)S(1)}, bf16[32,4096]{1,0:T(8,128)(2,1)S(1)}, u32[]{:S(2)}, u32[]{:S(2)}) collective-permute-start(bf16[32,4096]{1,0:T(8,128)(2,1)S(1)} %collective-permute-done.6.refs_11_), channel_id=1, source_target_pairs={{0,16},{1,17},{2,18},{3,19},{4,20},{5,21},{6,22},{7,23},{8,24},{9,... | collective-permute-start | bytes 786440 | tf_op jit(solution)/shard_map/ppermute | solution.py:238
  25.5 11.1 %collective-permute-start.12 = (bf16[32,4096]{1,0:T(8,128)(2,1)S(1)}, bf16[32,4096]{1,0:T(8,128)(2,1)S(1)}, u32[]{:S(2)}, u32[]{:S(2)}) collective-permute-start(bf16[32,4096]{1,0:T(8,128)(2,1)S(1)} %collective-permute-done.10.refs_15_), channel_id=1, source_target_pairs={{0,1},{1,0},{2,3},{3,2},{4,5},{5,4},{6,7},{7,6},{8,9},{9,8},{10,11... | collective-permute-start | bytes 786440 | tf_op jit(solution)/shard_map/ppermute | solution.py:238
  27.3 9.3 %collective-permute-start.4 = (bf16[32,4096]{1,0:T(8,128)(2,1)S(1)}, bf16[32,4096]{1,0:T(8,128)(2,1)S(1)}, u32[]{:S(2)}, u32[]{:S(2)}) collective-permute-start(bf16[32,4096]{1,0:T(8,128)(2,1)S(1)} %collective-permute-done.2.refs_7_), channel_id=1, source_target_pairs={{0,1},{1,0},{2,3},{3,2},{4,5},{5,4},{6,7},{7,6},{8,9},{9,8},{10,11... | collective-permute-start | bytes 786440 | tf_op jit(solution)/shard_map/ppermute | solution.py:238
  27.4 9.7 %collective-permute-start.8 = (bf16[32,4096]{1,0:T(8,128)(2,1)S(1)}, bf16[32,4096]{1,0:T(8,128)(2,1)S(1)}, u32[]{:S(2)}, u32[]{:S(2)}) collective-permute-start(bf16[32,4096]{1,0:T(8,128)(2,1)S(1)} %collective-permute-done.6.refs_11_), channel_id=1, source_target_pairs={{0,1},{1,0},{2,3},{3,2},{4,5},{5,4},{6,7},{7,6},{8,9},{9,8},{10,11... | collective-permute-start | bytes 786440 | tf_op jit(solution)/shard_map/ppermute | solution.py:238
  33.7 7.0 %collective-permute-start.1 = (bf16[64,4096]{1,0:T(8,128)(2,1)S(1)}, bf16[64,4096]{1,0:T(8,128)(2,1)S(1)}, u32[]{:S(2)}, u32[]{:S(2)}) collective-permute-start(bf16[64,4096]{1,0:T(8,128)(2,1)S(1)} %bitcast.46), channel_id=1, source_target_pairs={{0,1},{1,0},{2,3},{3,2},{4,5},{5,4},{6,7},{7,6},{8,9},{9,8},{10,11... | collective-permute-start | bytes 1572872 | tf_op jit(solution)/shard_map/ppermute | solution.py:238
  36.5 4.1 %collective-permute-start.13 = (bf16[32,4096]{1,0:T(8,128)(2,1)S(1)}, bf16[32,4096]{1,0:T(8,128)(2,1)}, u32[]{:S(2)}, u32[]{:S(2)}) collective-permute-start(bf16[32,4096]{1,0:T(8,128)(2,1)S(1)} %collective-permute-done.11.refs_16_), channel_id=1, source_target_pairs={{0,1},{1,0},{2,3},{3,2},{4,5},{5,4},{6,7},{7,6},{8,9},{9,8},{10,11... | collective-permute-start | bytes 786440 | tf_op jit(solution)/shard_map/ppermute | solution.py:238
  36.6 4.1 %collective-permute-start.5 = (bf16[32,4096]{1,0:T(8,128)(2,1)S(1)}, bf16[32,4096]{1,0:T(8,128)(2,1)}, u32[]{:S(2)}, u32[]{:S(2)}) collective-permute-start(bf16[32,4096]{1,0:T(8,128)(2,1)S(1)} %collective-permute-done.3.refs_8_), channel_id=1, source_target_pairs={{0,1},{1,0},{2,3},{3,2},{4,5},{5,4},{6,7},{7,6},{8,9},{9,8},{10,11... | collective-permute-start | bytes 786440 | tf_op jit(solution)/shard_map/ppermute | solution.py:238
  37.2 3.4 %collective-permute-start.9 = (bf16[32,4096]{1,0:T(8,128)(2,1)}, bf16[32,4096]{1,0:T(8,128)(2,1)}, u32[]{:S(2)}, u32[]{:S(2)}) collective-permute-start(bf16[32,4096]{1,0:T(8,128)(2,1)} %copy-done.8), channel_id=1, source_target_pairs={{0,1},{1,0},{2,3},{3,2},{4,5},{5,4},{6,7},{7,6},{8,9},{9,8},{10,11... | collective-permute-start | bytes 786440 | tf_op jit(solution)/shard_map/ppermute | solution.py:238
  48.6 21.3 %collective-permute-start.17 = (bf16[4,2,128,128]{3,2,1,0:T(8,128)(2,1)}, bf16[4,2,128,128]{3,2,1,0:T(8,128)(2,1)S(1)}, u32[]{:S(2)}, u32[]{:S(2)}) collective-permute-start(bf16[4,2,128,128]{3,2,1,0:T(8,128)(2,1)} %project.1.refs_4_), channel_id=1, source_target_pairs={{0,4},{1,5},{2,6},{3,7},{4,8},{5,9},{6,10},{7,11},{8,12},{9,13},{1... | collective-permute-start | bytes 786440 | tf_op jit(solution)/shard_map/ppermute | solution.py:238
  50.8 20.4 %collective-permute-start.21 = (bf16[4,2,128,128]{3,2,1,0:T(8,128)(2,1)}, bf16[4,2,128,128]{3,2,1,0:T(8,128)(2,1)S(1)}, u32[]{:S(2)}, u32[]{:S(2)}) collective-permute-start(bf16[4,2,128,128]{3,2,1,0:T(8,128)(2,1)} %project.1.refs_4_), channel_id=1, source_target_pairs={{0,8},{1,9},{2,10},{3,11},{4,12},{5,13},{6,14},{7,15},{16,24},{17,... | collective-permute-start | bytes 786440 | tf_op jit(solution)/shard_map/ppermute | solution.py:238
  52.1 19.3 %collective-permute-start.25 = (bf16[4,2,128,128]{3,2,1,0:T(8,128)(2,1)}, bf16[4,2,128,128]{3,2,1,0:T(8,128)(2,1)S(1)}, u32[]{:S(2)}, u32[]{:S(2)}) collective-permute-start(bf16[4,2,128,128]{3,2,1,0:T(8,128)(2,1)} %project.1.refs_4_), channel_id=1, source_target_pairs={{0,12},{1,13},{2,14},{3,15},{16,28},{17,29},{18,30},{19,31}} | collective-permute-start | bytes 786440 | tf_op jit(solution)/shard_map/ppermute | solution.py:238
  52.8 19.8 %collective-permute-start.15 = (bf16[4,2,128,128]{3,2,1,0:T(8,128)(2,1)}, bf16[4,2,128,128]{3,2,1,0:T(8,128)(2,1)S(1)}, u32[]{:S(2)}, u32[]{:S(2)}) collective-permute-start(bf16[4,2,128,128]{3,2,1,0:T(8,128)(2,1)} %project.1.refs_4_), channel_id=1, source_target_pairs={{0,2},{1,3},{2,0},{3,1},{4,6},{5,7},{6,4},{7,5},{8,10},{9,11},{10,... | collective-permute-start | bytes 786440 | tf_op jit(solution)/shard_map/ppermute | solution.py:238
  54.1 20.6 %collective-permute-start.14 = (bf16[4,2,128,128]{3,2,1,0:T(8,128)(2,1)}, bf16[4,2,128,128]{3,2,1,0:T(8,128)(2,1)S(1)}, u32[]{:S(2)}, u32[]{:S(2)}) collective-permute-start(bf16[4,2,128,128]{3,2,1,0:T(8,128)(2,1)} %project.1.refs_4_), channel_id=1, source_target_pairs={{0,1},{1,0},{2,3},{3,2},{4,5},{5,4},{6,7},{7,6},{8,9},{9,8},{10,11... | collective-permute-start | bytes 786440 | tf_op jit(solution)/shard_map/ppermute | solution.py:238
  69.9 6.6 %collective-permute-start.19 = (bf16[4,2,128,128]{3,2,1,0:T(8,128)(2,1)S(1)}, bf16[4,2,128,128]{3,2,1,0:T(8,128)(2,1)S(1)}, u32[]{:S(2)}, u32[]{:S(2)}) collective-permute-start(bf16[4,2,128,128]{3,2,1,0:T(8,128)(2,1)S(1)} %collective-permute-done.17.refs_8_), channel_id=1, source_target_pairs={{0,2},{1,3},{2,0},{3,1},{4,6},{5,7},{6,4},{7,5},{8,10},{9,11},{10,... | collective-permute-start | bytes 786440 | tf_op jit(solution)/shard_map/ppermute | solution.py:238
  71.1 11.0 %collective-permute-start.23 = (bf16[4,2,128,128]{3,2,1,0:T(8,128)(2,1)S(1)}, bf16[4,2,128,128]{3,2,1,0:T(8,128)(2,1)S(1)}, u32[]{:S(2)}, u32[]{:S(2)}) collective-permute-start(bf16[4,2,128,128]{3,2,1,0:T(8,128)(2,1)S(1)} %collective-permute-done.21.refs_12_), channel_id=1, source_target_pairs={{0,2},{1,3},{2,0},{3,1},{4,6},{5,7},{6,4},{7,5},{8,10},{9,11},{10,... | collective-permute-start | bytes 786440 | tf_op jit(solution)/shard_map/ppermute | solution.py:238
  71.4 16.4 %collective-permute-start.27 = (bf16[4,2,128,128]{3,2,1,0:T(8,128)(2,1)S(1)}, bf16[4,2,128,128]{3,2,1,0:T(8,128)(2,1)S(1)}, u32[]{:S(2)}, u32[]{:S(2)}) collective-permute-start(bf16[4,2,128,128]{3,2,1,0:T(8,128)(2,1)S(1)} %collective-permute-done.25.refs_16_), channel_id=1, source_target_pairs={{0,2},{1,3},{2,0},{3,1},{4,6},{5,7},{6,4},{7,5},{8,10},{9,11},{10,... | collective-permute-start | bytes 786440 | tf_op jit(solution)/shard_map/ppermute | solution.py:238
  72.6 17.2 %collective-permute-start.16 = (bf16[4,2,128,128]{3,2,1,0:T(8,128)(2,1)S(1)}, bf16[4,2,128,128]{3,2,1,0:T(8,128)(2,1)S(1)}, u32[]{:S(2)}, u32[]{:S(2)}) collective-permute-start(bf16[4,2,128,128]{3,2,1,0:T(8,128)(2,1)S(1)} %collective-permute-done.15.refs_6_), channel_id=1, source_target_pairs={{0,1},{1,0},{2,3},{3,2},{4,5},{5,4},{6,7},{7,6},{8,9},{9,8},{10,11... | collective-permute-start | bytes 786440 | tf_op jit(solution)/shard_map/ppermute | solution.py:238
  74.6 15.3 %collective-permute-start.18 = (bf16[4,2,128,128]{3,2,1,0:T(8,128)(2,1)S(1)}, bf16[4,2,128,128]{3,2,1,0:T(8,128)(2,1)S(1)}, u32[]{:S(2)}, u32[]{:S(2)}) collective-permute-start(bf16[4,2,128,128]{3,2,1,0:T(8,128)(2,1)S(1)} %collective-permute-done.17.refs_8_), channel_id=1, source_target_pairs={{0,1},{1,0},{2,3},{3,2},{4,5},{5,4},{6,7},{7,6},{8,9},{9,8},{10,11... | collective-permute-start | bytes 786440 | tf_op jit(solution)/shard_map/ppermute | solution.py:238
  76.5 19.2 %collective-permute-start.22 = (bf16[4,2,128,128]{3,2,1,0:T(8,128)(2,1)S(1)}, bf16[4,2,128,128]{3,2,1,0:T(8,128)(2,1)S(1)}, u32[]{:S(2)}, u32[]{:S(2)}) collective-permute-start(bf16[4,2,128,128]{3,2,1,0:T(8,128)(2,1)S(1)} %collective-permute-done.21.refs_12_), channel_id=1, source_target_pairs={{0,1},{1,0},{2,3},{3,2},{4,5},{5,4},{6,7},{7,6},{8,9},{9,8},{10,11... | collective-permute-start | bytes 786440 | tf_op jit(solution)/shard_map/ppermute | solution.py:238
  82.1 13.6 %collective-permute-start.26 = (bf16[4,2,128,128]{3,2,1,0:T(8,128)(2,1)S(1)}, bf16[4,2,128,128]{3,2,1,0:T(8,128)(2,1)S(1)}, u32[]{:S(2)}, u32[]{:S(2)}) collective-permute-start(bf16[4,2,128,128]{3,2,1,0:T(8,128)(2,1)S(1)} %collective-permute-done.25.refs_16_), channel_id=1, source_target_pairs={{0,1},{1,0},{2,3},{3,2},{4,5},{5,4},{6,7},{7,6},{8,9},{9,8},{10,11... | collective-permute-start | bytes 786440 | tf_op jit(solution)/shard_map/ppermute | solution.py:238
  87.8 8.0 %collective-permute-start.20 = (bf16[4,2,128,128]{3,2,1,0:T(8,128)(2,1)S(1)}, bf16[4,2,128,128]{3,2,1,0:T(8,128)(2,1)S(1)}, u32[]{:S(2)}, u32[]{:S(2)}) collective-permute-start(bf16[4,2,128,128]{3,2,1,0:T(8,128)(2,1)S(1)} %collective-permute-done.19.refs_10_), channel_id=1, source_target_pairs={{0,1},{1,0},{2,3},{3,2},{4,5},{5,4},{6,7},{7,6},{8,9},{9,8},{10,11... | collective-permute-start | bytes 786440 | tf_op jit(solution)/shard_map/ppermute | solution.py:238
  89.9 6.0 %collective-permute-start.24 = (bf16[4,2,128,128]{3,2,1,0:T(8,128)(2,1)S(1)}, bf16[4,2,128,128]{3,2,1,0:T(8,128)(2,1)}, u32[]{:S(2)}, u32[]{:S(2)}) collective-permute-start(bf16[4,2,128,128]{3,2,1,0:T(8,128)(2,1)S(1)} %collective-permute-done.23.refs_14_), channel_id=1, source_target_pairs={{0,1},{1,0},{2,3},{3,2},{4,5},{5,4},{6,7},{7,6},{8,9},{9,8},{10,11... | collective-permute-start | bytes 786440 | tf_op jit(solution)/shard_map/ppermute | solution.py:238
  89.9 5.9 %collective-permute-start.28 = (bf16[4,2,128,128]{3,2,1,0:T(8,128)(2,1)S(1)}, bf16[4,2,128,128]{3,2,1,0:T(8,128)(2,1)}, u32[]{:S(2)}, u32[]{:S(2)}) collective-permute-start(bf16[4,2,128,128]{3,2,1,0:T(8,128)(2,1)S(1)} %collective-permute-done.27.refs_18_), channel_id=1, source_target_pairs={{0,1},{1,0},{2,3},{3,2},{4,5},{5,4},{6,7},{7,6},{8,9},{9,8},{10,11... | collective-permute-start | bytes 786440 | tf_op jit(solution)/shard_map/ppermute | solution.py:238
  (23 other events, 237.5 us)

commit v2 on v0

v2 whole, which is shorter than its diff:
```python
import math

import jax
import jax.numpy as jnp
from jax import lax
from jax.experimental import pallas as pl
from jax.experimental.pallas import tpu as pltpu
from jax.sharding import PartitionSpec as P

KVH = 4
QPK = 8
HD = 128
AXES = ("groups", "node")
MASKED = -1e30
EXP2_SCALE = HD ** (-0.5) * math.log2(math.e)
VMEM_LIMIT = 48 * 1024 * 1024

ANY = pl.BlockSpec(memory_space=pl.ANY)
IN_SMEM = pl.BlockSpec(memory_space=pltpu.SMEM)
IN_VMEM = pl.BlockSpec(memory_space=pltpu.VMEM)


def scalars(*values):
    return jnp.stack([jnp.asarray(v).astype(jnp.int32) for v in values])


def rope_tables(positions):
    half = HD // 2
    freqs = 500000.0 ** (-(jnp.arange(half).astype(jnp.float32) * 2.0) / HD)
    angle = positions.astype(jnp.float32)[:, None] * freqs[None, :]
    return jnp.cos(angle), jnp.sin(angle)


def attend_kernel(rows, chunk, n_q, n_kv, place_ref, start_ref, *refs):
    queries = refs[:n_q]
    arrays = refs[n_q : n_q + n_kv]
    outs = refs[n_q + n_kv : 2 * n_q + n_kv]
    kv, qv, whole, acc, stat_m, stat_l, bias, sem, qsem = refs[2 * n_q + n_kv :]
    part_rows = queries[0].shape[0]
    length = arrays[0].shape[0]

    def q_copy(i):
        column = pl.multiple_of(place_ref[4 + 2 * i], HD)
        return pltpu.make_async_copy(
            queries[i].at[:, pl.ds(column, QPK * HD)],
            qv.at[pl.ds(pl.multiple_of(place_ref[3 + 2 * i], part_rows), part_rows)],
            qsem.at[i],
        )

    def kv_copy(i):
        base = 3 + 2 * n_q + 3 * i
        return pltpu.make_async_copy(
            arrays[i],
            kv.at[place_ref[base + 1], pl.ds(pl.multiple_of(place_ref[base + 2], length), length)],
            sem.at[i],
        )

    for i in range(n_q):
        q_copy(i).start()
    for i in range(n_kv):

        @pl.when(place_ref[3 + 2 * n_q + 3 * i] == 1)
        def _():
            kv_copy(i).start()

    stat_m[...] = jnp.full_like(stat_m, MASKED)
    stat_l[...] = jnp.zeros_like(stat_l)
    acc[...] = jnp.zeros_like(acc)
    for i in range(n_q):
        q_copy(i).wait()
    for i in range(n_kv):

        @pl.when(place_ref[3 + 2 * n_q + 3 * i] == 1)
        def _():
            kv_copy(i).wait()

    starts = start_ref[...]
    q_pos = place_ref[2] + lax.broadcasted_iota(jnp.int32, (chunk, rows), 1)

    @pl.loop(place_ref[0], place_ref[1])
    def _(t):
        begin = pl.multiple_of(t * chunk, chunk)
        k_pos = begin + lax.broadcasted_iota(jnp.int32, (chunk, rows), 0)
        bias[...] = jnp.where((k_pos <= q_pos) & (k_pos >= starts), 0.0, MASKED)
        keys = kv[0, pl.ds(begin, chunk), :]
        values_t = kv[1, pl.ds(begin, chunk), :].T
        for h in range(QPK):
            score = lax.dot_general(
                keys,
                qv[:, h * HD : (h + 1) * HD],
                (((1,), (1,)), ((), ())),
                preferred_element_type=jnp.float32,
            )
            score = score + bias[...]
            old = stat_m[h : h + 1, :]
            top = jnp.maximum(old, jnp.max(score, axis=0, keepdims=True))
            expo = jnp.exp2((score - top) * EXP2_SCALE)
            factor = jnp.exp2((old - top) * EXP2_SCALE)
            stat_m[h : h + 1, :] = top
            stat_l[h : h + 1, :] = stat_l[h : h + 1, :] * factor + jnp.sum(
                expo, axis=0, keepdims=True
            )
            part = jnp.dot(
                values_t, expo.astype(jnp.bfloat16), preferred_element_type=jnp.float32
            )
            acc[h] = acc[h] * factor + part

    for h in range(QPK):
        done = acc[h] / stat_l[h : h + 1, :]
        whole[:, h * HD : (h + 1) * HD] = done.T.astype(jnp.bfloat16)
    for i in range(n_q):
        at = pl.multiple_of(place_ref[3 + 2 * i], part_rows)
        outs[i][...] = whole[pl.ds(at, part_rows), :]


def attend_plan(doc_ids, first_row, rows, chunk):
    docs = lax.dynamic_slice_in_dim(doc_ids, first_row, rows)
    starts = jnp.sum((doc_ids[None, :] < docs[:, None]).astype(jnp.int32), axis=1)
    end = (first_row + rows + chunk - 1) // chunk
    return starts.reshape(1, rows), starts[0] // chunk, end


def attend(place, starts, queries, arrays, tokens, chunk):
    rows = starts.shape[1]
    n_q, n_kv = len(queries), len(arrays)
    part_rows = queries[0].shape[0]
    return pl.pallas_call(
        lambda *refs: attend_kernel(rows, chunk, n_q, n_kv, *refs),
        out_shape=[jax.ShapeDtypeStruct((part_rows, QPK * HD), jnp.bfloat16)] * n_q,
        in_specs=[IN_SMEM, IN_VMEM] + [ANY] * (n_q + n_kv),
        out_specs=[IN_VMEM] * n_q,
        scratch_shapes=[
            pltpu.VMEM((2, tokens, HD), jnp.bfloat16),
            pltpu.VMEM((rows, QPK * HD), jnp.bfloat16),
            pltpu.VMEM((rows, QPK * HD), jnp.bfloat16),
            pltpu.VMEM((QPK, HD, rows), jnp.float32),
            pltpu.VMEM((QPK, rows), jnp.float32),
            pltpu.VMEM((QPK, rows), jnp.float32),
            pltpu.VMEM((chunk, rows), jnp.float32),
            pltpu.SemaphoreType.DMA((n_kv,)),
            pltpu.SemaphoreType.DMA((n_q,)),
        ],
        compiler_params=pltpu.CompilerParams(vmem_limit_bytes=VMEM_LIMIT),
        cost_estimate=pl.CostEstimate(
            flops=4 * rows * tokens * HD * QPK,
            bytes_accessed=4 * 1024 * 1024,
            transcendentals=rows * tokens * QPK,
        ),
        name="attend",
    )(place, starts, *queries, *arrays)


def project_kernel(rows, n_hidden, n_pieces, place_ref, cos_ref, sin_ref, *refs):
    hidden = refs[:n_hidden]
    pieces = refs[n_hidden : n_hidden + n_pieces]
    out_ref = refs[n_hidden + n_pieces]
    hbuf, wbuf, hsem, wsem = refs[n_hidden + n_pieces + 1 :]

    def w_copy(i):
        size = pieces[i].shape[0]
        at = pl.multiple_of(place_ref[2 + n_hidden + 2 * i], size)
        return pltpu.make_async_copy(pieces[i], wbuf.at[pl.ds(at, size)], wsem.at[i])

    def h_copy(i):
        return pltpu.make_async_copy(hidden[i], hbuf.at[i], hsem.at[i])

    for i in range(n_pieces):

        @pl.when(place_ref[1 + n_hidden + 2 * i] == 1)
        def _():
            w_copy(i).start()

    for i in range(n_hidden):
        h_copy(i).start()
    for i in range(n_pieces):

        @pl.when(place_ref[1 + n_hidden + 2 * i] == 1)
        def _():
            w_copy(i).wait()

    rotate = place_ref[0] == 1
    for i in range(n_hidden):
        h_copy(i).wait()
        block = place_ref[1 + i]
        head = lax.dot_general(
            hbuf[i], wbuf[...], (((1,), (1,)), ((), ())), preferred_element_type=jnp.float32
        )
        turned = head * cos_ref[block] + pltpu.roll(head, HD // 2, 1) * sin_ref[block]
        out_ref[pl.ds(pl.multiple_of(block * rows, rows), rows), :] = jnp.where(
            rotate, turned, head
        ).astype(jnp.bfloat16)


def project(place, cos, sin, hidden, pieces):
    rows, depth = hidden[0].shape
    n = len(hidden)
    return pl.pallas_call(
        lambda *refs: project_kernel(rows, n, len(pieces), *refs),
        out_shape=jax.ShapeDtypeStruct((n * rows, HD), jnp.bfloat16),
        in_specs=[IN_SMEM, IN_VMEM, IN_VMEM] + [ANY] * (n + len(pieces)),
        out_specs=IN_VMEM,
        scratch_shapes=[
            pltpu.VMEM((n, rows, depth), jnp.bfloat16),
            pltpu.VMEM((HD, depth), jnp.bfloat16),
            pltpu.SemaphoreType.DMA((n,)),
            pltpu.SemaphoreType.DMA((len(pieces),)),
        ],
        compiler_params=pltpu.CompilerParams(vmem_limit_bytes=VMEM_LIMIT),
        cost_estimate=pl.CostEstimate(
            flops=2 * n * rows * depth * HD,
            bytes_accessed=5 * 1024 * 1024,
            transcendentals=0,
        ),
        name="project",
    )(place, cos, sin, *hidden, *pieces)


def join_kernel(place_ref, *refs):
    n = len(refs) - 2
    out_ref, sem = refs[n:]
    copies = []
    for i in range(n):
        width = refs[i].shape[1]
        at = pl.multiple_of(place_ref[i], width)
        copies.append(
            pltpu.make_async_copy(refs[i], out_ref.at[:, pl.ds(at, width)], sem.at[i])
        )
    for c in copies:
        c.start()
    for c in copies:
        c.wait()


def join(place, parts, shape):
    return pl.pallas_call(
        join_kernel,
        out_shape=jax.ShapeDtypeStruct(shape, parts[0].dtype),
        in_specs=[IN_SMEM] + [ANY] * len(parts),
        out_specs=ANY,
        scratch_shapes=[pltpu.SemaphoreType.DMA((len(parts),))],
        name="join",
    )(place, *parts)


def by_planes(hidden, queries, kv_weight, doc_ids):
    rows = hidden.shape[0]
    tokens = doc_ids.shape[0]
    width = kv_weight.shape[1]
    x = lax.axis_index("groups")
    node = lax.axis_index("node")
    z, y, c = node // 4, (node // 2) % 2, node % 2
    low = z % 2

    def hop(fn):
        pairs = []
        for i in range(32):
            to = fn(i // 16, (i // 4) % 4, (i // 2) % 2, i % 2)
            if to is not None:
                pairs.append((i, ((to[0] * 4 + to[1]) * 2 + to[2]) * 2 + to[3]))
        return lambda v: lax.ppermute(v, AXES, pairs)

    to_core = hop(lambda x, z, y, c: (x, z, y, 1 - c))
    to_y = hop(lambda x, z, y, c: (x, z, 1 - y, c))
    to_x = hop(lambda x, z, y, c: (1 - x, z, y, c))
    to_x_late = hop(lambda x, z, y, c: (1 - x, z, y, c) if c != z % 2 else None)
    near = hop(lambda x, z, y, c: (x, z ^ 1, y, z % 2) if c == x else None)
    far = hop(lambda x, z, y, c: (x, z ^ (2 + c), y, z % 2))
    pair = hop(lambda x, z, y, c: (x, z ^ 1, y, c))
    up = {
        k: hop(lambda x, z, y, c, k=k: (x, z + k, y, c) if z + k < 4 else None) for k in (1, 2, 3)
    }

    weight = kv_weight.T
    part = width // 2
    far_0 = far(lax.dynamic_slice_in_dim(weight, x * part, part, 0))
    near_0 = near(weight)
    hidden_y = to_y(hidden)
    hidden_c = to_core(hidden)
    weight_c = to_core(weight)

    positions = z * 4 * rows + jnp.arange(4 * rows)
    cosine, sine = rope_tables(positions)
    cos = jnp.concatenate([cosine, cosine], axis=1).reshape(4, rows, HD)
    sin = jnp.concatenate([-sine, sine], axis=1).reshape(4, rows, HD)
    chunk = math.gcd(tokens, 256)
    first_row = (4 * z + 2 * y) * rows
    starts, first_chunk, end_chunk = attend_plan(doc_ids, first_row, 2 * rows, chunk)
    blocks = [2 * y + c, 2 * y + 1 - c, 2 * (1 - y) + c, 2 * (1 - y) + 1 - c]
    own = (c == low).astype(jnp.int32)
    place_a = scalars(
        z < 2, *blocks, own, c * width, own, (1 - c) * width,
        1 - own, x * width, 1 - own, (1 - x) * width,
    )
    side = (1 - own) * width
    place_b = scalars(
        z >= 2, *blocks, 1, side + x * part, 1, side + (1 - x) * part,
        1, width - side + x * part, 1, width - side + (1 - x) * part,
    )
    half_cols = queries.shape[1] // 2
    places_q = []
    for head in (y, 1 - y):
        at = head * QPK * HD
        values = [first_chunk, end_chunk, first_row]
        values += [c * rows, c * half_cols + at, (1 - c) * rows, at]
        for k in range(4):
            plane = z - k
            used = (plane >= 0) & ((plane + 1) * 4 * rows > first_chunk * chunk)
            plane = jnp.maximum(plane, 0)
            values += [used, plane // 2, plane * 4 * rows]
            values += [used, 1 - plane // 2, plane * 4 * rows]
        places_q.append(scalars(*values))
    place_out = scalars(
        (2 * c + y) * QPK * HD, (2 * c + 1 - y) * QPK * HD,
        (2 * (1 - c) + y) * QPK * HD, (2 * (1 - c) + 1 - y) * QPK * HD,
    )
    q_away = lax.dynamic_slice_in_dim(queries, (1 - c) * half_cols, half_cols, 1)
    (far_0, cos, sin, starts, place_a, place_b, places_q, place_out, q_away) = (
        lax.optimization_barrier(
            (far_0, cos, sin, starts, place_a, place_b, places_q, place_out, q_away)
        )
    )
    q_here = to_core(q_away)

    far_1 = pair(far_0)
    far_0x = to_x(far_0)
    near_x = to_x_late(near_0)
    far_1x = to_x(far_1)
    hidden_yc = to_core(hidden_y)
    plane_hidden = [hidden, hidden_c, hidden_y, hidden_yc]
    kv_a = project(place_a, cos, sin, plane_hidden, [weight, weight_c, near_0, near_x])
    kv_b = project(place_b, cos, sin, plane_hidden, [far_0, far_0x, far_1, far_1x])

    mine, others = [], []
    a_up = [kv_a] + [up[k](kv_a) for k in (1, 2, 3)]
    b_up = [kv_b] + [up[k](kv_b) for k in (1, 2, 3)]
    for k in range(4):
        mine += [a_up[k], b_up[k]]
        others += [to_y(a_up[k]), to_y(b_up[k])]
    keep_0, away_0 = attend(places_q[0], starts, [queries, q_here], mine, tokens, chunk)
    back_0 = to_core(away_0)
    keep_1, away_1 = attend(places_q[1], starts, [queries, q_here], others, tokens, chunk)
    back_1 = to_core(away_1)
    return join(place_out, [keep_0, keep_1, back_0, back_1], queries.shape)


def by_gathers(hidden, queries, kv_weight, doc_ids):
    rows = hidden.shape[0]
    tokens = doc_ids.shape[0]
    me = lax.axis_index("node")
    whole = lax.all_gather(kv_weight, "node", axis=1, tiled=True)
    projected = jnp.dot(hidden, whole, preferred_element_type=jnp.float32)
    split = whole.shape[1] // 2
    cosine, sine = rope_tables(me * rows + jnp.arange(rows))
    keys = projected[:, :split].reshape(rows, KVH, HD)
    a, b = keys[..., : HD // 2], keys[..., HD // 2 :]
    cosine, sine = cosine[:, None, :], sine[:, None, :]
    keys = jnp.concatenate([a * cosine - b * sine, b * cosine + a * sine], axis=-1)
    both = jnp.concatenate([keys, projected[:, split:].reshape(rows, KVH, HD)], axis=1)
    both = both.astype(jnp.bfloat16).transpose(1, 0, 2)
    whole = lax.all_gather(both, "node", axis=1, tiled=True)
    chunk = math.gcd(tokens, 256)
    starts, first_chunk, end_chunk = attend_plan(doc_ids, me * rows, rows, chunk)
    outs = []
    for g in range(KVH):
        place = scalars(
            first_chunk, end_chunk, me * rows, 0, g * QPK * HD, 1, 0, 0, 1, 1, 0
        )
        outs += attend(place, starts, [queries], [whole[g], whole[KVH + g]], tokens, chunk)
    return jnp.concatenate(outs, axis=1)


def solution(mesh):
    planes = mesh.shape["groups"] == 2 and mesh.shape["node"] == 16
    in_specs = (P(AXES, None), P(AXES, None), P(None, "node"), P("groups"))
    return jax.shard_map(
        by_planes if planes else by_gathers,
        mesh=mesh,
        in_specs=in_specs,
        out_specs=P(AXES, None),
        check_vma=False,
    )
```

time: 223 us -> 165 us (0.74)
  waiting for transfers between devices: 138 us -> 46.4 us
  Pallas kernels: 0 us -> 76.1 us
  starting transfers between devices: 0.08 us -> 27.8 us
  matrix products: 27.6 us -> 0 us
  local copies, waits for them, and re-layouts: 30.3 us -> 7.59 us
  between operations: 13.2 us -> 2.82 us
  other arithmetic: 12.8 us -> 3.7 us
    all_gather x3 -> x0, waiting for transfers between devices: 137 us -> none  [the longest x1 75.9 us: per_device(): whole_weight = lax.all_gather(kv_weight, 'node', axis=1, tiled=True)]
    pallas_call x0 -> x5, Pallas kernels: none -> 76.1 us  [the longest x1 33.6 us: join(): pl.pallas_call(join_kernel, out_shape=jax.ShapeDtypeStruct(shape, parts[0...]
    ppermute x0 -> x27, waiting for transfers between devices: none -> 46.4 us  [hop(): return lambda v: lax.ppermute(v, AXES, pairs)]
    ppermute x0 -> x27, starting transfers between devices: none -> 27.8 us  [hop(): return lambda v: lax.ppermute(v, AXES, pairs)]
    dot_general x11 -> x0, matrix products: 27.6 us -> none  [the longest x5 15.1 us: update(): jnp.einsum('qgpk,kgh->qgph', expo.astype(jnp.bfloat16), value_block, pref...]
    cond x19 -> x0, local copies, waits for them, and re-layouts: 9.82 us -> none
    reduce_sum x5 -> x1, other arithmetic: 8.83 us -> 0.36 us  [attend_plan(): jnp.sum((doc_ids[None, :] < docs[:, None]).astype(jnp.int32), axis=1)]
    dynamic_slice x10 -> x3, local copies, waits for them, and re-layouts: 9.68 us -> 2.57 us  [the longest x1 1.66 us: by_planes(): far_0 = far(lax.dynamic_slice_in_dim(weight, x * part, part, 0))]
  transfers between devices with their start and end apart: 3 -> 27, of which waited for: 3 -> 8; matrix products, arithmetic and copies ran while one was open for 9% -> 4% of each run, Pallas kernels for 0% -> 26%
where the time goes in v2:
time: 165 us; the launch traced here: 164 us
  Pallas kernels  76.1 us (46%)
  waiting for transfers between devices  46.4 us (28%)
  starting transfers between devices  27.8 us (17%)
  local copies, waits for them, and re-layouts  7.59 us (5%)
  other arithmetic  3.7 us (2%)
  between operations  2.82 us (2%)
    ppermute x27, waiting for transfers between devices, hop(): return lambda v: lax.ppermute(v, AXES, pairs)  46.4 us
    pallas_call x1, Pallas kernels, join(): pl.pallas_call(join_kernel, out_shape=jax.ShapeDtypeStruct(shape, parts[0...  33.6 us
    pallas_call x2, Pallas kernels, attend(): pl.pallas_call(lambda *refs: attend_kernel(rows, chunk, n_q, n_kv, *refs)...  33.1 us
    ppermute x27, starting transfers between devices, hop(): return lambda v: lax.ppermute(v, AXES, pairs)  27.8 us
    pallas_call x2, Pallas kernels, project(): pl.pallas_call(lambda *refs: project_kernel(rows, n, len(pieces), *refs),...  9.35 us
    unnamed x26, local copies, waits for them, and re-layouts  4.09 us
  transfers between devices with their start and end apart: 27, of which 8 were waited for; matrix products, arithmetic and copies ran while one was open for 4% of the time, Pallas kernels for 26%

profile of v2, /device:TPU:29, one launch (start us, length us, event | category | flops | bytes accessed | tf_op | source)
XLA Modules:
  0.0 164.4 jit_solution(3195639150994695127)
XLA Ops:
  0.2 1.0 collective-permute-start.2
  1.2 1.5 collective-permute-start.6
  2.7 1.7 %dynamic-slice_bitcast_fusion = bf16[32,4096]{1,0:T(8,128)(2,1)} fusion(bf16[4096,64]{0,1:T(8,128)(2,1)} %param.6, s32[]{:T(128)S(6)} %select_n.61), kind=kLoop, calls=%fused_computation.5 | loop fusion | bytes 524292 | tf_op jit(solution)/shard_map/dynamic_slice | solution.py:275
  4.3 1.9 %fusion = (f32[4,128,64]{2,1,0:T(8,128)}, f32[4,128,64]{2,1,0:T(8,128)}, f32[4,128,64]{2,1,0:T(8,128)}) fusion(f32[64]{0:T(128)S(1)} %multiply_power_fusion, f32[4,128]{1,0:T(4,128)S(1)} %add_convert_fusion), kind=kLoop, calls=%fused_computation.6 | loop fusion | flops 65536 | bytes 395520 | tf_op jit(solution)/shard_map/neg | solution.py:284
  6.2 18.0 %collective-permute-done.3.refs_5_ = bf16[128,4096]{1,0:T(8,128)(2,1)S(1)} collective-permute-done((bf16[128,4096]{1,0:T(8,128)(2,1)}, bf16[128,4096]{1,0:T(8,128)(2,1)S(1)}, u32[]{:S(2)}, u32[]{:S(2)}) %collective-permute-start.3) | collective-permute-done | bytes 1048608 | tf_op jit(solution)/shard_map/ppermute | solution.py:260
  24.2 1.5 collective-permute-start.4
  25.8 0.8 constant_dynamic-slice_fusion
  26.6 0.9 pad_maximum_fusion
  28.0 1.5 collective-permute-start.7
  33.5 1.9 %collective-permute-start.9 = (bf16[32,4096]{1,0:T(8,128)(2,1)}, bf16[32,4096]{1,0:T(8,128)(2,1)S(1)}, u32[]{:S(2)}, u32[]{:S(2)}) collective-permute-start(bf16[32,4096]{1,0:T(8,128)(2,1)} %collective-permute-done.refs_7_), channel_id=1, source_target_pairs={{0,4},{1,5},{2,6},{3,7},{4,0},{5,1},{6,2},{7,3},{8,12},{9,13},{10,... | collective-permute-start | bytes 786440 | tf_op jit(solution)/shard_map/ppermute | solution.py:260
  35.7 5.9 %collective-permute-done.9.refs_9_ = bf16[32,4096]{1,0:T(8,128)(2,1)S(1)} collective-permute-done((bf16[32,4096]{1,0:T(8,128)(2,1)}, bf16[32,4096]{1,0:T(8,128)(2,1)S(1)}, u32[]{:S(2)}, u32[]{:S(2)}) %collective-permute-start.9) | collective-permute-done | bytes 262176 | tf_op jit(solution)/shard_map/ppermute | solution.py:260
  41.9 1.2 collective-permute-start.10
  43.1 0.9 copy-done.1
  44.0 1.0 copy-done.2
  45.1 4.7 %project.2.refs_4_ = bf16[512,128]{1,0:T(8,128)(2,1)S(1)} custom-call(s32[13]{0:T(128)S(1)} %stack.223.refs_0_, f32[4,128,128]{2,1,0:T(8,128)S(1)} %get-tuple-element.24.refs_1_, f32[4,128,128]{2,1,0:T(8,128)S(1)} %copy-done.1, bf16[128,4096]{1,0:T(8,128)(2,1)S(1)} %copy-done, bf16[128,4096]{1,0:T(8,128)(2,1)S(1)} %collective-permute-done.2.refs_4_, ...), custom_call_target="tpu_custom_call" | custom-call | flops 536870912 | bytes 5242880 | tf_op jit(solution)/shard_map/project/pallas_call | solution.py:197
  49.8 1.4 collective-permute-start.11
  51.3 2.6 %collective-permute-done.10.refs_10_ = bf16[32,4096]{1,0:T(8,128)(2,1)S(1)} collective-permute-done((bf16[32,4096]{1,0:T(8,128)(2,1)S(1)}, bf16[32,4096]{1,0:T(8,128)(2,1)S(1)}, u32[]{:S(2)}, u32[]{:S(2)}) %collective-permute-start.10) | collective-permute-done | bytes 262176 | tf_op jit(solution)/shard_map/ppermute | solution.py:260
  53.9 4.6 %project.3.refs_5_ = bf16[512,128]{1,0:T(8,128)(2,1)S(1)} custom-call(s32[13]{0:T(128)S(1)} %stack.230.refs_0_, f32[4,128,128]{2,1,0:T(8,128)S(1)} %get-tuple-element.24.refs_1_, f32[4,128,128]{2,1,0:T(8,128)S(1)} %copy-done.1, bf16[128,4096]{1,0:T(8,128)(2,1)S(1)} %copy-done, bf16[128,4096]{1,0:T(8,128)(2,1)S(1)} %collective-permute-done.2.refs_4_, ...), custom_call_target="tpu_custom_call" | custom-call | flops 536870912 | bytes 5242880 | tf_op jit(solution)/shard_map/project/pallas_call | solution.py:197
  58.5 1.3 collective-permute-start.12
  59.8 1.3 collective-permute-start.13
  61.1 1.3 collective-permute-start.14
  62.4 1.3 collective-permute-start.15
  63.7 1.3 collective-permute-start.16
  65.8 14.3 %collective-permute-done.13.refs_8_ = bf16[512,128]{1,0:T(8,128)(2,1)S(1)} collective-permute-done((bf16[512,128]{1,0:T(8,128)(2,1)S(1)}, bf16[512,128]{1,0:T(8,128)(2,1)S(1)}, u32[]{:S(2)}, u32[]{:S(2)}) %collective-permute-start.13) | collective-permute-done | bytes 131104 | tf_op jit(solution)/shard_map/ppermute | solution.py:260
  80.3 2.9 %collective-permute-done.14.refs_9_ = bf16[512,128]{1,0:T(8,128)(2,1)S(1)} collective-permute-done((bf16[512,128]{1,0:T(8,128)(2,1)S(1)}, bf16[512,128]{1,0:T(8,128)(2,1)S(1)}, u32[]{:S(2)}, u32[]{:S(2)}) %collective-permute-start.14) | collective-permute-done | bytes 131104 | tf_op jit(solution)/shard_map/ppermute | solution.py:260
  83.4 1.2 collective-permute-start.20
  84.9 1.2 collective-permute-start.22
  87.6 16.6 %attend.2 = (bf16[128,1024]{1,0:T(8,128)(2,1)S(1)}, bf16[128,1024]{1,0:T(8,128)(2,1)S(1)}) custom-call(s32[31]{0:T(128)S(1)} %stack.258.refs_0_, s32[1,256]{1,0:T(1,128)S(1)} %bitcast.53, bf16[128,4096]{1,0:T(8,128)(2,1)S(1)} %copy-done.6, bf16[128,2048]{1,0:T(8,128)(2,1)S(1)} %collective-permute-done.1.refs_3_, bf16[512,128]{1,0:T(8,128)(2,1)S(1)} %project.2.refs_4_, ...), custom_call_target="tpu_custom_call" | custom-call | flops 2147483648 | bytes 4194304 | tf_op jit(solution)/shard_map/attend/pallas_call | solution.py:127
  104.9 6.4 %collective-permute-start.25 = (bf16[128,1024]{1,0:T(8,128)(2,1)S(1)}, bf16[128,1024]{1,0:T(8,128)(2,1)S(1)}, u32[]{:S(2)}, u32[]{:S(2)}) collective-permute-start(bf16[128,1024]{1,0:T(8,128)(2,1)S(1)} %get-tuple-element.31), channel_id=1, source_target_pairs={{0,1},{1,0},{2,3},{3,2},{4,5},{5,4},{6,7},{7,6},{8,9},{9,8},{10,11... | collective-permute-start | bytes 786440 | tf_op jit(solution)/shard_map/ppermute | solution.py:260
  111.3 16.6 %attend.3 = (bf16[128,1024]{1,0:T(8,128)(2,1)S(1)}, bf16[128,1024]{1,0:T(8,128)(2,1)S(1)}) custom-call(s32[31]{0:T(128)S(1)} %stack.261.refs_0_, s32[1,256]{1,0:T(1,128)S(1)} %bitcast.54, bf16[128,4096]{1,0:T(8,128)(2,1)S(1)} %copy-done.6, bf16[128,2048]{1,0:T(8,128)(2,1)S(1)} %collective-permute-done.1.refs_3_, ...), custom_call_target="tpu_custom_call" | custom-call | flops 2147483648 | bytes 4194304 | tf_op jit(solution)/shard_map/attend/pallas_call | solution.py:127
  128.6 1.5 collective-permute-done.26.refs_3_
  130.8 33.6 %join.1 = bf16[128,4096]{1,0:T(8,128)(2,1)} custom-call(s32[4]{0:T(128)} %pad_add_fusion.place_ref, bf16[128,1024]{1,0:T(8,128)(2,1)} %copy-done.3, bf16[128,1024]{1,0:T(8,128)(2,1)} %copy-done.4, bf16[128,1024]{1,0:T(8,128)(2,1)} %copy-done.10, bf16[128,1024]{1,0:T(8,128)(2,1)} %copy-done.11), custom_call_target="tpu_custom_call" | custom-call | tf_op jit(solution)/shard_map/join/pallas_call | solution.py:235
  (67 shorter events, 7.7 us)
Async XLA Ops:
  0.0 25.8 %copy-start.5 = (bf16[128,4096]{1,0:T(8,128)(2,1)S(1)}, bf16[128,4096]{1,0:T(8,128)(2,1)}, u32[]{:S(2)}) copy-start(bf16[128,4096]{1,0:T(8,128)(2,1)} %refs_2_.3) | copy-start | bytes 3145732
  0.0 24.2 %collective-permute-start.3 = (bf16[128,4096]{1,0:T(8,128)(2,1)}, bf16[128,4096]{1,0:T(8,128)(2,1)S(1)}, u32[]{:S(2)}, u32[]{:S(2)}) collective-permute-start(bf16[128,4096]{1,0:T(8,128)(2,1)} %refs_3_.3), channel_id=1, source_target_pairs={{0,2},{1,3},{2,0},{3,1},{4,6},{5,7},{6,4},{7,5},{8,10},{9,11},{10,... | collective-permute-start | bytes 3145736 | tf_op jit(solution)/shard_map/ppermute | solution.py:260
  0.2 41.6 %collective-permute-start.2 = (bf16[128,4096]{1,0:T(8,128)(2,1)}, bf16[128,4096]{1,0:T(8,128)(2,1)S(1)}, u32[]{:S(2)}, u32[]{:S(2)}) collective-permute-start(bf16[128,4096]{1,0:T(8,128)(2,1)} %refs_3_.3), channel_id=1, source_target_pairs={{0,1},{1,0},{2,3},{3,2},{4,5},{5,4},{6,7},{7,6},{8,9},{9,8},{10,11... | collective-permute-start | bytes 3145736 | tf_op jit(solution)/shard_map/ppermute | solution.py:260
  1.2 34.3 %collective-permute-start.5 = (bf16[64,4096]{1,0:T(8,128)(2,1)}, bf16[64,4096]{1,0:T(8,128)(2,1)}, u32[]{:S(2)}, u32[]{:S(2)}) collective-permute-start(bf16[64,4096]{1,0:T(8,128)(2,1)} %bitcast.50), channel_id=1, source_target_pairs={{0,1},{1,0},{2,3},{3,2},{4,5},{5,4},{6,7},{7,6},{8,9},{9,8},{10,11... | collective-permute-start | bytes 1572872 | tf_op jit(solution)/shard_map/ppermute | solution.py:260
  1.2 26.8 %collective-permute-start.6 = (bf16[64,4096]{1,0:T(8,128)(2,1)}, bf16[64,4096]{1,0:T(8,128)(2,1)}, u32[]{:S(2)}, u32[]{:S(2)}) collective-permute-start(bf16[64,4096]{1,0:T(8,128)(2,1)} %bitcast.51), channel_id=1, source_target_pairs={{0,4},{2,6},{4,1},{6,3},{8,12},{10,14},{12,9},{14,11},{17,20},{19,... | collective-permute-start | bytes 1572872 | tf_op jit(solution)/shard_map/ppermute | solution.py:260
  4.3 29.2 %collective-permute-start = (bf16[32,4096]{1,0:T(8,128)(2,1)}, bf16[32,4096]{1,0:T(8,128)(2,1)}, u32[]{:S(2)}, u32[]{:S(2)}) collective-permute-start(bf16[32,4096]{1,0:T(8,128)(2,1)} %dynamic-slice_bitcast_fusion), channel_id=1, source_target_pairs={{0,8},{1,12},{2,10},{3,14},{4,13},{5,9},{6,15},{7,11},{8,0},{9,4},... | collective-permute-start | bytes 786440 | tf_op jit(solution)/shard_map/ppermute | solution.py:260
  6.2 20.4 %copy-start.8 = (f32[4,128,64]{2,1,0:T(8,128)S(1)}, f32[4,128,64]{2,1,0:T(8,128)}, u32[]{:S(2)}) copy-start(f32[4,128,64]{2,1,0:T(8,128)} %get-tuple-element.34) | copy-start | bytes 393220
  6.2 20.4 %copy-start.9 = (f32[4,128,64]{2,1,0:T(8,128)S(1)}, f32[4,128,64]{2,1,0:T(8,128)}, u32[]{:S(2)}) copy-start(f32[4,128,64]{2,1,0:T(8,128)} %get-tuple-element.35) | copy-start | bytes 393220
  6.2 21.3 %copy-start.12 = (s32[2048]{0:T(1024)S(1)}, s32[2048]{0:T(1024)}, u32[]{:S(2)}) copy-start(s32[2048]{0:T(1024)} %param.7) | copy-start | bytes 24580
  24.2 18.8 %collective-permute-start.4 = (bf16[128,4096]{1,0:T(8,128)(2,1)S(1)}, bf16[128,4096]{1,0:T(8,128)(2,1)}, u32[]{:S(2)}, u32[]{:S(2)}) collective-permute-start(bf16[128,4096]{1,0:T(8,128)(2,1)S(1)} %collective-permute-done.3.refs_5_), channel_id=1, source_target_pairs={{0,1},{1,0},{2,3},{3,2},{4,5},{5,4},{6,7},{7,6},{8,9},{9,8},{10,11... | collective-permute-start | bytes 3145736 | tf_op jit(solution)/shard_map/ppermute | solution.py:260
  28.0 15.1 %collective-permute-start.7 = (bf16[64,4096]{1,0:T(8,128)(2,1)}, bf16[64,4096]{1,0:T(8,128)(2,1)}, u32[]{:S(2)}, u32[]{:S(2)}) collective-permute-start(bf16[64,4096]{1,0:T(8,128)(2,1)} %collective-permute-done.6.refs_9_), channel_id=1, source_target_pairs={{1,17},{3,19},{4,20},{6,22},{9,25},{11,27},{12,28},{14,30},{17,1},... | collective-permute-start | bytes 1572872 | tf_op jit(solution)/shard_map/ppermute | solution.py:260
  33.5 8.0 %collective-permute-start.9 = (bf16[32,4096]{1,0:T(8,128)(2,1)}, bf16[32,4096]{1,0:T(8,128)(2,1)S(1)}, u32[]{:S(2)}, u32[]{:S(2)}) collective-permute-start(bf16[32,4096]{1,0:T(8,128)(2,1)} %collective-permute-done.refs_7_), channel_id=1, source_target_pairs={{0,4},{1,5},{2,6},{3,7},{4,0},{5,1},{6,2},{7,3},{8,12},{9,13},{10,... | collective-permute-start | bytes 786440 | tf_op jit(solution)/shard_map/ppermute | solution.py:260
  35.5 27.0 %collective-permute-start.1 = (bf16[128,2048]{1,0:T(8,128)(2,1)}, bf16[128,2048]{1,0:T(8,128)(2,1)S(1)}, u32[]{:S(2)}, u32[]{:S(2)}) collective-permute-start(bf16[128,2048]{1,0:T(8,128)(2,1)} %constant_dynamic-slice_fusion), channel_id=1, source_target_pairs={{0,1},{1,0},{2,3},{3,2},{4,5},{5,4},{6,7},{7,6},{8,9},{9,8},{10,11... | collective-permute-start | bytes 1572872 | tf_op jit(solution)/shard_map/ppermute | solution.py:260
  41.6 9.7 %collective-permute-start.8 = (bf16[32,4096]{1,0:T(8,128)(2,1)}, bf16[32,4096]{1,0:T(8,128)(2,1)S(1)}, u32[]{:S(2)}, u32[]{:S(2)}) collective-permute-start(bf16[32,4096]{1,0:T(8,128)(2,1)} %collective-permute-done.refs_7_), channel_id=1, source_target_pairs={{0,16},{1,17},{2,18},{3,19},{4,20},{5,21},{6,22},{7,23},{8,24},{9,... | collective-permute-start | bytes 786440 | tf_op jit(solution)/shard_map/ppermute | solution.py:260
  41.9 12.0 %collective-permute-start.10 = (bf16[32,4096]{1,0:T(8,128)(2,1)S(1)}, bf16[32,4096]{1,0:T(8,128)(2,1)S(1)}, u32[]{:S(2)}, u32[]{:S(2)}) collective-permute-start(bf16[32,4096]{1,0:T(8,128)(2,1)S(1)} %collective-permute-done.9.refs_9_), channel_id=1, source_target_pairs={{0,16},{1,17},{2,18},{3,19},{4,20},{5,21},{6,22},{7,23},{8,24},{9,... | collective-permute-start | bytes 786440 | tf_op jit(solution)/shard_map/ppermute | solution.py:260
  49.8 37.8 %copy-start.6 = (bf16[128,4096]{1,0:T(8,128)(2,1)S(1)}, bf16[128,4096]{1,0:T(8,128)(2,1)}, u32[]{:S(2)}) copy-start(bf16[128,4096]{1,0:T(8,128)(2,1)} %refs_2_.3) | copy-start | bytes 3145732
  49.8 13.9 %collective-permute-start.11 = (bf16[512,128]{1,0:T(8,128)(2,1)S(1)}, bf16[512,128]{1,0:T(8,128)(2,1)S(1)}, u32[]{:S(2)}, u32[]{:S(2)}) collective-permute-start(bf16[512,128]{1,0:T(8,128)(2,1)S(1)} %project.2.refs_4_), channel_id=1, source_target_pairs={{0,4},{1,5},{2,6},{3,7},{4,8},{5,9},{6,10},{7,11},{8,12},{9,13},{1... | collective-permute-start | bytes 393224 | tf_op jit(solution)/shard_map/ppermute | solution.py:260
  58.5 7.0 %collective-permute-start.12 = (bf16[512,128]{1,0:T(8,128)(2,1)S(1)}, bf16[512,128]{1,0:T(8,128)(2,1)S(1)}, u32[]{:S(2)}, u32[]{:S(2)}) collective-permute-start(bf16[512,128]{1,0:T(8,128)(2,1)S(1)} %project.3.refs_5_), channel_id=1, source_target_pairs={{0,4},{1,5},{2,6},{3,7},{4,8},{5,9},{6,10},{7,11},{8,12},{9,13},{1... | collective-permute-start | bytes 393224 | tf_op jit(solution)/shard_map/ppermute | solution.py:260
  59.8 20.3 %collective-permute-start.13 = (bf16[512,128]{1,0:T(8,128)(2,1)S(1)}, bf16[512,128]{1,0:T(8,128)(2,1)S(1)}, u32[]{:S(2)}, u32[]{:S(2)}) collective-permute-start(bf16[512,128]{1,0:T(8,128)(2,1)S(1)} %project.2.refs_4_), channel_id=1, source_target_pairs={{0,8},{1,9},{2,10},{3,11},{4,12},{5,13},{6,14},{7,15},{16,24},{17,... | collective-permute-start | bytes 393224 | tf_op jit(solution)/shard_map/ppermute | solution.py:260
  61.1 22.1 %collective-permute-start.14 = (bf16[512,128]{1,0:T(8,128)(2,1)S(1)}, bf16[512,128]{1,0:T(8,128)(2,1)S(1)}, u32[]{:S(2)}, u32[]{:S(2)}) collective-permute-start(bf16[512,128]{1,0:T(8,128)(2,1)S(1)} %project.3.refs_5_), channel_id=1, source_target_pairs={{0,8},{1,9},{2,10},{3,11},{4,12},{5,13},{6,14},{7,15},{16,24},{17,... | collective-permute-start | bytes 393224 | tf_op jit(solution)/shard_map/ppermute | solution.py:260
  62.4 21.0 %collective-permute-start.15 = (bf16[512,128]{1,0:T(8,128)(2,1)S(1)}, bf16[512,128]{1,0:T(8,128)(2,1)S(1)}, u32[]{:S(2)}, u32[]{:S(2)}) collective-permute-start(bf16[512,128]{1,0:T(8,128)(2,1)S(1)} %project.2.refs_4_), channel_id=1, source_target_pairs={{0,12},{1,13},{2,14},{3,15},{16,28},{17,29},{18,30},{19,31}} | collective-permute-start | bytes 393224 | tf_op jit(solution)/shard_map/ppermute | solution.py:260
  63.7 20.9 %collective-permute-start.16 = (bf16[512,128]{1,0:T(8,128)(2,1)S(1)}, bf16[512,128]{1,0:T(8,128)(2,1)S(1)}, u32[]{:S(2)}, u32[]{:S(2)}) collective-permute-start(bf16[512,128]{1,0:T(8,128)(2,1)S(1)} %project.3.refs_5_), channel_id=1, source_target_pairs={{0,12},{1,13},{2,14},{3,15},{16,28},{17,29},{18,30},{19,31}} | collective-permute-start | bytes 393224 | tf_op jit(solution)/shard_map/ppermute | solution.py:260
  65.5 19.3 %collective-permute-start.17 = (bf16[512,128]{1,0:T(8,128)(2,1)S(1)}, bf16[512,128]{1,0:T(8,128)(2,1)S(1)}, u32[]{:S(2)}, u32[]{:S(2)}) collective-permute-start(bf16[512,128]{1,0:T(8,128)(2,1)S(1)} %project.2.refs_4_), channel_id=1, source_target_pairs={{0,2},{1,3},{2,0},{3,1},{4,6},{5,7},{6,4},{7,5},{8,10},{9,11},{10,... | collective-permute-start | bytes 393224 | tf_op jit(solution)/shard_map/ppermute | solution.py:260
  80.1 6.1 %collective-permute-start.18 = (bf16[512,128]{1,0:T(8,128)(2,1)S(1)}, bf16[512,128]{1,0:T(8,128)(2,1)S(1)}, u32[]{:S(2)}, u32[]{:S(2)}) collective-permute-start(bf16[512,128]{1,0:T(8,128)(2,1)S(1)} %project.3.refs_5_), channel_id=1, source_target_pairs={{0,2},{1,3},{2,0},{3,1},{4,6},{5,7},{6,4},{7,5},{8,10},{9,11},{10,... | collective-permute-start | bytes 393224 | tf_op jit(solution)/shard_map/ppermute | solution.py:260
  83.2 3.8 %collective-permute-start.19 = (bf16[512,128]{1,0:T(8,128)(2,1)S(1)}, bf16[512,128]{1,0:T(8,128)(2,1)S(1)}, u32[]{:S(2)}, u32[]{:S(2)}) collective-permute-start(bf16[512,128]{1,0:T(8,128)(2,1)S(1)} %collective-permute-done.11.refs_6_), channel_id=1, source_target_pairs={{0,2},{1,3},{2,0},{3,1},{4,6},{5,7},{6,4},{7,5},{8,10},{9,11},{10,... | collective-permute-start | bytes 393224 | tf_op jit(solution)/shard_map/ppermute | solution.py:260
  83.4 21.5 %collective-permute-start.20 = (bf16[512,128]{1,0:T(8,128)(2,1)S(1)}, bf16[512,128]{1,0:T(8,128)(2,1)S(1)}, u32[]{:S(2)}, u32[]{:S(2)}) collective-permute-start(bf16[512,128]{1,0:T(8,128)(2,1)S(1)} %collective-permute-done.12.refs_7_), channel_id=1, source_target_pairs={{0,2},{1,3},{2,0},{3,1},{4,6},{5,7},{6,4},{7,5},{8,10},{9,11},{10,... | collective-permute-start | bytes 393224 | tf_op jit(solution)/shard_map/ppermute | solution.py:260
  84.6 26.7 %collective-permute-start.21 = (bf16[512,128]{1,0:T(8,128)(2,1)S(1)}, bf16[512,128]{1,0:T(8,128)(2,1)S(1)}, u32[]{:S(2)}, u32[]{:S(2)}) collective-permute-start(bf16[512,128]{1,0:T(8,128)(2,1)S(1)} %collective-permute-done.13.refs_8_), channel_id=1, source_target_pairs={{0,2},{1,3},{2,0},{3,1},{4,6},{5,7},{6,4},{7,5},{8,10},{9,11},{10,... | collective-permute-start | bytes 393224 | tf_op jit(solution)/shard_map/ppermute | solution.py:260
  84.9 26.4 %collective-permute-start.22 = (bf16[512,128]{1,0:T(8,128)(2,1)S(1)}, bf16[512,128]{1,0:T(8,128)(2,1)S(1)}, u32[]{:S(2)}, u32[]{:S(2)}) collective-permute-start(bf16[512,128]{1,0:T(8,128)(2,1)S(1)} %collective-permute-done.14.refs_9_), channel_id=1, source_target_pairs={{0,2},{1,3},{2,0},{3,1},{4,6},{5,7},{6,4},{7,5},{8,10},{9,11},{10,... | collective-permute-start | bytes 393224 | tf_op jit(solution)/shard_map/ppermute | solution.py:260
  86.1 25.2 %collective-permute-start.23 = (bf16[512,128]{1,0:T(8,128)(2,1)S(1)}, bf16[512,128]{1,0:T(8,128)(2,1)S(1)}, u32[]{:S(2)}, u32[]{:S(2)}) collective-permute-start(bf16[512,128]{1,0:T(8,128)(2,1)S(1)} %collective-permute-done.15.refs_10_), channel_id=1, source_target_pairs={{0,2},{1,3},{2,0},{3,1},{4,6},{5,7},{6,4},{7,5},{8,10},{9,11},{10,... | collective-permute-start | bytes 393224 | tf_op jit(solution)/shard_map/ppermute | solution.py:260
  87.0 24.3 %collective-permute-start.24 = (bf16[512,128]{1,0:T(8,128)(2,1)S(1)}, bf16[512,128]{1,0:T(8,128)(2,1)S(1)}, u32[]{:S(2)}, u32[]{:S(2)}) collective-permute-start(bf16[512,128]{1,0:T(8,128)(2,1)S(1)} %collective-permute-done.16.refs_11_), channel_id=1, source_target_pairs={{0,2},{1,3},{2,0},{3,1},{4,6},{5,7},{6,4},{7,5},{8,10},{9,11},{10,... | collective-permute-start | bytes 393224 | tf_op jit(solution)/shard_map/ppermute | solution.py:260
  104.9 23.7 %collective-permute-start.25 = (bf16[128,1024]{1,0:T(8,128)(2,1)S(1)}, bf16[128,1024]{1,0:T(8,128)(2,1)S(1)}, u32[]{:S(2)}, u32[]{:S(2)}) collective-permute-start(bf16[128,1024]{1,0:T(8,128)(2,1)S(1)} %get-tuple-element.31), channel_id=1, source_target_pairs={{0,1},{1,0},{2,3},{3,2},{4,5},{5,4},{6,7},{7,6},{8,9},{9,8},{10,11... | collective-permute-start | bytes 786440 | tf_op jit(solution)/shard_map/ppermute | solution.py:260
  128.6 1.5 collective-permute-start.26
  (8 other events, 42.5 us)
